TPU v7x, 256 devices: a whole 4x4x8 slice. The times are simulated.
256 devices in a mesh: ctx: 32 (over z_lo, y, core), head: 8 (over z_hi, x).
Axes of the slice: x: 4, y: 4, z: 8 (z_hi: 2, z_lo: 4; z = z_hi * 4 + z_lo), core: 2. Of those that a mesh axis runs over, the one named last changes fastest.
Arguments:
- hidden_states: bfloat16 [4096, 7168], P('ctx', 'head'), may hold values from -384 to 384
- down_query: bfloat16 [7168, 1536], P('head'), may hold values from -0.0625 to 0.0625
- down_latent: bfloat16 [7168, 576], P('head'), may hold values from -0.0625 to 0.0625
- query_gain: float32 [1536], replicated, may hold values from 0.1 to 1.9
- latent_gain: float32 [512], replicated, may hold values from 0.1 to 1.9
- up_query: bfloat16 [1536, 12288], P(None, 'head'), may hold values from -0.15625 to 0.15625
- up_key: bfloat16 [512, 8192], P(None, 'head'), may hold values from -0.375 to 0.375
- up_value: bfloat16 [512, 8192], P(None, 'head'), may hold values from -0.75 to 0.75
- owner_table: int32 [64], replicated, may hold values from 0 to 63, each once
Outputs:
- attended: bfloat16 [4096, 8192], P('ctx', 'head')
Inputs may be any that keep to these rules, and one draw needn't show every extreme that they name: Block b of the sequence, positions 64 * b to 64 * b + 63, lies in token rows 64 * owner_table[b] to 64 * owner_table[b] + 63; each row block holds exactly one sequence block.
All inputs are finite; a program needn't handle non-finite values.
Results may differ from a plain program's by a relative error of at most 0.035.
Values may be sent and summed in bfloat16 or wider, within the bound.
No kernel may reach another device: no remote copies, remote signals or barrier semaphores. Data moves between devices by JAX's collectives and lax.ppermute only.
A program may use at most 128 MiB of HBM per device.

v0:
```python
import functools
import math

import jax
import jax.numpy as jnp
from jax import lax
from jax.experimental import pallas as pl
from jax.experimental.pallas import tpu as pltpu
from jax.sharding import PartitionSpec as P

RD = 64
NOPE = 128
VD = 128
KVL = 512
BLK = 64
LANES = 128
WIDE = KVL + LANES
CHUNK = 32
PACK = CHUNK * (KVL + RD) // LANES
QPACK = 12
TILE = 512
SPAN = 256
NEG = -1e30
SCALE = 1.0 / math.sqrt(NOPE + RD)
LOG2E = math.log2(math.e)
NX, NY, NZ, NZL, NC = 4, 4, 8, 4, 2
AXES = ("ctx", "head")
OFFSETS = (0, -1, 1, 2)
CONTRACT_LAST = (((1,), (1,)), ((), ()))
VMEM = pl.BlockSpec(memory_space=pltpu.VMEM)
SMEM = pl.BlockSpec(memory_space=pltpu.SMEM)
FAR = pl.BlockSpec(memory_space=pltpu.HBM)


def angles(positions):
    half_width = RD // 2
    step_index = jnp.arange(half_width).astype(jnp.float32)
    frequency = jnp.exp(step_index * (-math.log(10000.0) / half_width))
    return positions.astype(jnp.float32)[..., None] * frequency


def rotary_tables(positions):
    table = angles(positions)
    cosines, sines = jnp.cos(table), jnp.sin(table)
    return (
        jnp.concatenate([cosines, cosines], axis=-1),
        jnp.concatenate([-sines, sines], axis=-1),
    )


def block_positions(owner_table, row_index, block_rows):
    slot_index = row_index // block_rows
    block_count = owner_table.shape[0]
    match_table = (owner_table[None, :] == slot_index[:, None]).astype(jnp.int32)
    block_index = jnp.sum(match_table * jnp.arange(block_count, dtype=jnp.int32)[None, :], axis=1)
    return block_index * block_rows + row_index % block_rows


def flat(x, y, z, c):
    ctx = ((z % NZL) * NY + y) * NC + c
    return ctx * (2 * NX) + (z // NZL) * NX + x


def send(value, move):
    pairs = []
    for x in range(NX):
        for y in range(NY):
            for z in range(NZ):
                for c in range(NC):
                    tx, ty, tz, tc = move(x, y, z, c)
                    pairs.append((flat(x, y, z, c), flat(tx % NX, ty % NY, tz % NZ, tc)))
    return lax.ppermute(value, AXES, pairs)


def along_x(step):
    return lambda x, y, z, c: (x + step, y, z, c)


def pair_x(shift):
    return lambda x, y, z, c: (x + (1 if (x + shift) % 2 == 0 else -1), y, z, c)


def pair_order(x):
    partner = (x + NX - 1 + 2 * (x & 1)) & (NX - 1)
    return [x, x + 1 - 2 * (x & 1), partner, partner + 1 - 2 * (partner & 1)]


def step_z(z, step):
    return z - step if abs(step) == 2 and z % 2 else z + step


def along_first(step):
    return lambda x, y, z, c: (x, y + step, z, c) if c == 0 else (x, y, step_z(z, step), c)


def along_second(step):
    return lambda x, y, z, c: (x, y, step_z(z, step), c) if c == 0 else (x, y + step, z, c)


def other_half(x, y, z, c):
    return (x, y, z + NZL, c)


def other_core(x, y, z, c):
    return (x, y, z, 1 - c)


def gather_ring(value, along):
    return [value] + [send(value, along(-offset)) for offset in OFFSETS[1:]]


def kernel_call(kernel, out_shape, in_specs, scratch, flops, moved, limit=32):
    return pl.pallas_call(
        kernel,
        out_shape=out_shape,
        in_specs=in_specs,
        out_specs=jax.tree.map(lambda _: VMEM, out_shape),
        scratch_shapes=scratch,
        compiler_params=pltpu.CompilerParams(vmem_limit_bytes=limit * 2**20),
        cost_estimate=pl.CostEstimate(flops=flops, bytes_accessed=moved, transcendentals=0),
    )


def key_down_kernel(x_ref, hidden_far, weight_far, *refs):
    pieces, (hidden, weight, part, sems) = refs[:NX], refs[NX:]
    half = weight.shape[0] // 2
    loads = [pltpu.make_async_copy(hidden_far, hidden, sems.at[0])]
    for index in range(2):
        rows = pl.ds(index * half, half)
        loads.append(
            pltpu.make_async_copy(weight_far.at[rows], weight.at[rows], sems.at[1 + index])
        )
    for load in loads:
        load.start()
    for load in loads:
        load.wait()
    part[...] = lax.dot_general(
        hidden[...], weight[...], CONTRACT_LAST, preferred_element_type=jnp.float32
    )
    for step, piece in enumerate(pieces):
        start = pl.multiple_of(((x_ref[0] + step) & (NX - 1)) * CHUNK, CHUNK)
        rows = part[pl.ds(start, CHUNK), :]
        for tile in range(KVL // LANES):
            piece[tile * CHUNK : (tile + 1) * CHUNK] = rows[:, tile * LANES : (tile + 1) * LANES]
        rope = rows[:, KVL:]
        piece[KVL // LANES * CHUNK : PACK] = jnp.concatenate(
            [rope[: CHUNK // 2], rope[CHUNK // 2 :]], axis=1
        )


def key_down(x_index, hidden, weight):
    rows = hidden.shape[0]
    return kernel_call(
        key_down_kernel,
        [jax.ShapeDtypeStruct((PACK, LANES), jnp.float32)] * NX,
        [SMEM, FAR, FAR],
        [
            pltpu.VMEM(hidden.shape, hidden.dtype),
            pltpu.VMEM(weight.shape, weight.dtype),
            pltpu.VMEM((rows, weight.shape[0]), jnp.float32),
            pltpu.SemaphoreType.DMA((3,)),
        ],
        2 * rows * weight.size,
        2 * weight.size,
        limit=63,
    )(x_index, hidden, weight)


def query_down_kernel(x_ref, hidden, weight, *refs):
    pieces, part = refs[:NX], refs[NX]
    part[...] = jnp.dot(hidden[...], weight[...], preferred_element_type=jnp.float32)
    for step, piece in enumerate(pieces):
        start = pl.multiple_of(((x_ref[0] + step) & (NX - 1)) * CHUNK, CHUNK)
        for tile in range(QPACK):
            piece[tile * CHUNK : (tile + 1) * CHUNK] = part[
                pl.ds(start, CHUNK), tile * LANES : (tile + 1) * LANES
            ]


def query_down(x_index, hidden, weight):
    rows = hidden.shape[0]
    return kernel_call(
        query_down_kernel,
        [jax.ShapeDtypeStruct((QPACK * CHUNK, LANES), jnp.float32)] * NX,
        [SMEM, VMEM, VMEM],
        [pltpu.VMEM((rows, weight.shape[1]), jnp.float32)],
        2 * rows * weight.size,
        2 * weight.size,
        limit=16,
    )(x_index, hidden, weight)


def sum_kernel(own, one, two, three, out):
    out[...] = own[...] + one[...] + two[...] + three[...]


def reduce_x(pieces):
    arrived = [send(pieces[step], along_x(step)) for step in (1, 2, 3)]
    return kernel_call(
        sum_kernel,
        jax.ShapeDtypeStruct(pieces[0].shape, jnp.float32),
        [VMEM] * 4,
        [],
        4 * pieces[0].size,
        16 * pieces[0].size,
    )(pieces[0], *arrived)


def join_kernel(rows, *refs):
    pieces, out = refs[:-1], refs[-1]
    for index, piece in enumerate(pieces):
        out[index * rows : (index + 1) * rows] = piece[:rows]


def join(pieces, rows):
    shape = (len(pieces) * rows, LANES)
    size = len(pieces) * rows * LANES
    return kernel_call(
        functools.partial(join_kernel, rows),
        jax.ShapeDtypeStruct(shape, pieces[0].dtype),
        [VMEM] * len(pieces),
        [],
        size,
        4 * size,
    )(*pieces)


def exchange_halves(values, lanes):
    half = RD // 2
    left = pltpu.roll(values, LANES - half, 1)
    right = pltpu.roll(values, half, 1)
    return jnp.where((lanes & half) == 0, left, right)


def norm_tiles(total, gain, out, start, count):
    tiles = [total[start + i * CHUNK : start + (i + 1) * CHUNK] for i in range(count)]
    squares = sum(tile * tile for tile in tiles)
    mean = jnp.sum(squares, axis=1, keepdims=True) * (1.0 / (count * LANES))
    factor = lax.rsqrt(mean + 1e-06)
    for index, tile in enumerate(tiles):
        out[start + index * CHUNK : start + (index + 1) * CHUNK] = (
            tile * factor * gain[index : index + 1, :]
        ).astype(out.dtype)


def key_norm_kernel(own, other, gain, cosines, sines, out):
    total = own[...] + other[...]
    norm_tiles(total, gain, out, 0, KVL // LANES)
    rope = total[KVL // LANES * CHUNK :]
    lanes = lax.broadcasted_iota(jnp.int32, rope.shape, 1)
    out[KVL // LANES * CHUNK :] = (
        rope * cosines[...] + exchange_halves(rope, lanes) * sines[...]
    ).astype(out.dtype)


def query_norm_kernel(own, other, gain, out):
    norm_tiles(own[...] + other[...], gain, out, 0, QPACK)


def query_kernel(x_ref, own, first, second, up_query, up_key, cosines, sines, out, rows):
    pair = 2 * (NOPE + RD)
    pairs = up_query.shape[1] // pair
    size = QPACK * CHUNK
    places = zip(pair_order(x_ref[0]), (own, first, second, second), (0, 0, 0, size))
    for place, piece, at in places:
        start = pl.multiple_of(place * CHUNK, CHUNK)
        for tile in range(QPACK):
            rows[pl.ds(start, CHUNK), tile * LANES : (tile + 1) * LANES] = piece[
                at + tile * CHUNK : at + (tile + 1) * CHUNK
            ]
    tokens = rows.shape[0]
    lanes = lax.broadcasted_iota(jnp.int32, (tokens, LANES), 1)
    for index in range(pairs):
        full = jnp.dot(
            rows[...],
            up_query[:, index * pair : (index + 1) * pair],
            preferred_element_type=jnp.float32,
        )
        first, second, third = (full[:, i * LANES : (i + 1) * LANES] for i in range(3))
        second_half, third_half = pltpu.roll(second, RD, 1), pltpu.roll(third, RD, 1)
        heads = (
            (first, second),
            (jnp.where(lanes < RD, second_half, third_half), third_half),
        )
        for offset, (nope, rope) in enumerate(heads):
            head = 2 * index + offset
            absorbed = lax.dot_general(
                nope.astype(jnp.bfloat16),
                up_key[:, head * NOPE : (head + 1) * NOPE],
                CONTRACT_LAST,
                preferred_element_type=jnp.float32,
            )
            out[head * tokens : (head + 1) * tokens, :KVL] = absorbed.astype(out.dtype)
            turned = rope * cosines[...] + exchange_halves(rope, lanes) * sines[...]
            out[head * tokens : (head + 1) * tokens, KVL:] = jnp.where(
                lanes < RD, turned, 0.0
            ).astype(out.dtype)


def attend_kernel(parts, first, last, *refs):
    refs = list(refs)
    queries, key_at, query_at = refs[:3]
    sources, refs = refs[3 : 3 + parts], refs[3 + parts :]
    if not first:
        (old_top, old_total, old_acc), refs = refs[:3], refs[3:]
    if last:
        up_value, out, refs = refs[0], refs[1], refs[2:]
    else:
        (new_top, new_total, new_acc), refs = refs[:3], refs[3:]
    keys, scores, acc = refs

    chunks = TILE // CHUNK
    for part, source in enumerate(sources):
        for chunk in range(chunks):
            to, at = part * TILE + chunk * CHUNK, chunk * PACK
            for tile in range(KVL // LANES):
                keys[to : to + CHUNK, tile * LANES : (tile + 1) * LANES] = source[
                    at + tile * CHUNK : at + (tile + 1) * CHUNK
                ]
            rope = source[at + KVL // LANES * CHUNK : at + PACK]
            keys[to : to + CHUNK // 2, KVL:] = rope
            keys[to + CHUNK // 2 : to + CHUNK, KVL:] = jnp.concatenate(
                [rope[:, RD:], rope[:, :RD]], axis=1
            )

    tokens = query_at.shape[0]
    rows_at = jnp.concatenate([query_at[...]] * (SPAN // tokens), axis=0)
    spans = queries.shape[0] // SPAN
    tops, totals, weights = {}, {}, {}

    def score(span, tile):
        view = slice(tile * TILE, (tile + 1) * TILE)
        value = lax.dot_general(
            queries[span * SPAN : (span + 1) * SPAN],
            keys[view],
            CONTRACT_LAST,
            preferred_element_type=jnp.float32,
        )
        value = jnp.where(key_at[:, view] <= rows_at, value, NEG)
        scores[span % 2, :, view] = value
        for lane in range(TILE // LANES):
            column = value[:, lane * LANES : (lane + 1) * LANES]
            tops[span] = jnp.maximum(tops[span], column) if span in tops else column

    def mix(span, tile):
        rows = slice(span * SPAN, (span + 1) * SPAN)
        view = slice(tile * TILE, (tile + 1) * TILE)
        if tile == 0:
            top = jnp.max(tops[span], axis=1, keepdims=True)
            if not first:
                before = old_top[rows, :1]
                top = jnp.maximum(top, before)
                weights[span] = jnp.exp2((before - top) * (SCALE * LOG2E))
            tops[span] = top
        terms = jnp.exp2((scores[span % 2, :, view] - tops[span]) * (SCALE * LOG2E))
        for lane in range(TILE // LANES):
            column = terms[:, lane * LANES : (lane + 1) * LANES]
            totals[span] = totals[span] + column if span in totals else column
        value = jnp.dot(
            terms.astype(jnp.bfloat16), keys[view, :KVL], preferred_element_type=jnp.float32
        )
        if tile > 0:
            value = acc[span % 2] + value
        elif not first:
            value = old_acc[rows] * weights[span] + value
        if tile < parts - 1:
            acc[span % 2] = value
            return
        total = jnp.sum(totals[span], axis=1, keepdims=True)
        if not first:
            total = total + old_total[rows, :1] * weights[span]
        if not last:
            new_acc[rows] = value
            new_top[rows] = jnp.broadcast_to(tops[span], (SPAN, LANES))
            new_total[rows] = jnp.broadcast_to(total, (SPAN, LANES))
            return
        latent_mix = (value / total).astype(jnp.bfloat16)
        for index in range(SPAN // tokens):
            head = span * (SPAN // tokens) + index
            columns = slice(head * VD, (head + 1) * VD)
            out[:, columns] = jnp.dot(
                latent_mix[index * tokens : (index + 1) * tokens],
                up_value[:, columns],
                preferred_element_type=jnp.float32,
            ).astype(out.dtype)

    for span in range(spans + 1):
        for tile in range(parts):
            if span < spans:
                score(span, tile)
            if span > 0:
                mix(span - 1, tile)


def attend(queries, key_at, query_at, sources, state=(), up_value=None):
    rows, parts = queries.shape[0], len(sources)
    tokens = query_at.shape[0]
    if up_value is not None:
        out_shape = jax.ShapeDtypeStruct((tokens, rows // tokens * VD), jnp.bfloat16)
    else:
        out_shape = [
            jax.ShapeDtypeStruct((rows, LANES), jnp.float32),
            jax.ShapeDtypeStruct((rows, LANES), jnp.float32),
            jax.ShapeDtypeStruct((rows, KVL), jnp.float32),
        ]
    operands = [queries, key_at, query_at, *sources, *state]
    specs = [VMEM] * len(operands)
    keys = parts * TILE
    scratch = [
        pltpu.VMEM((keys, WIDE), jnp.bfloat16),
        pltpu.VMEM((2, SPAN, keys), jnp.float32),
        pltpu.VMEM((2, SPAN, KVL), jnp.float32),
    ]
    if up_value is not None:
        operands.append(up_value)
        specs.append(VMEM)
    return kernel_call(
        functools.partial(attend_kernel, parts, not state, up_value is not None),
        out_shape,
        specs,
        scratch,
        2 * rows * keys * (KVL + WIDE),
        keys * WIDE * 4,
    )(*operands)


def chunk_rows(x, y, zl, core):
    ring = jnp.array(OFFSETS, jnp.int32)
    first, second = ring[None, :, None], ring[:, None, None]
    y_at = (y + jnp.where(core == 0, first, second)) % NY
    z_at = (zl + jnp.where(core == 0, second, first)) % NZL
    x_at = jnp.stack(pair_order(x))[None, None, :]
    return (((z_at * NY + y_at) * NC + core) * (NX * CHUNK) + x_at * CHUNK).reshape(-1)


def body(
    hidden_states,
    down_query,
    down_latent,
    query_gain,
    latent_gain,
    up_query,
    up_key,
    up_value,
    owner_table,
):
    tok_rows = hidden_states.shape[0]
    local_heads = up_key.shape[1] // NOPE
    ctx = lax.axis_index("ctx")
    head = lax.axis_index("head")
    x = head % NX
    c, y, zl = ctx % NC, (ctx // NC) % NY, ctx // (NC * NY)
    x_index = x.reshape(1)

    firsts = jnp.concatenate([chunk_rows(x, y, zl, c), chunk_rows(x, y, zl, 1 - c)])
    starts = block_positions(owner_table, firsts, BLK)
    key_at = (starts[:, None] + jnp.arange(CHUNK, dtype=jnp.int32)[None, :]).reshape(1, -1)
    own_rows = ctx * tok_rows + jnp.arange(tok_rows, dtype=jnp.int32)
    own_positions = block_positions(owner_table, own_rows, BLK)
    key_cos, key_sin = (
        jnp.concatenate([table[: CHUNK // 2], table[CHUNK // 2 :]], axis=1)
        for table in rotary_tables(starts[0] + jnp.arange(CHUNK, dtype=jnp.int32))
    )
    query_cos, query_sin = (
        jnp.concatenate([table, table], axis=1) for table in rotary_tables(own_positions)
    )

    key_half = reduce_x(key_down(x_index, hidden_states, down_latent.T))
    key_other = send(key_half, other_half)
    _, hidden_states = lax.optimization_barrier((key_half, hidden_states))
    query_pieces = query_down(x_index, hidden_states, down_query)
    key_pack = kernel_call(
        key_norm_kernel,
        jax.ShapeDtypeStruct((PACK, LANES), jnp.bfloat16),
        [VMEM] * 5,
        [],
        10 * PACK * LANES,
        10 * PACK * LANES,
    )(key_half, key_other, latent_gain.reshape(-1, LANES), key_cos, key_sin)
    key_pack, query_pieces = lax.optimization_barrier((key_pack, query_pieces))
    query_half = reduce_x(query_pieces)
    key_pair = join([key_pack, send(key_pack, pair_x(0))], PACK)
    key_own = join([key_pair, send(key_pair, pair_x(1))], 2 * PACK)
    key_own, query_half = lax.optimization_barrier((key_own, query_half))
    key_first = join(gather_ring(key_own, along_first), key_own.shape[0])

    near = [key_first] + [send(key_first, along_second(-offset)) for offset in OFFSETS[1:3]]

    query_rows = QPACK * CHUNK
    query_latent = kernel_call(
        query_norm_kernel,
        jax.ShapeDtypeStruct(query_half.shape, jnp.bfloat16),
        [VMEM] * 3,
        [],
        10 * query_half.size,
        10 * query_half.size,
    )(query_half, send(query_half, other_half), query_gain.reshape(-1, LANES))
    key_last, query_latent = lax.optimization_barrier((key_first, query_latent))
    near.append(send(key_last, along_second(-OFFSETS[3])))
    query_first = send(query_latent, pair_x(0))
    query_second = send(join([query_latent, query_first], query_rows), pair_x(1))
    queries = kernel_call(
        query_kernel,
        jax.ShapeDtypeStruct((local_heads * tok_rows, WIDE), jnp.bfloat16),
        [SMEM] + [VMEM] * 7,
        [pltpu.VMEM((tok_rows, up_query.shape[0]), jnp.bfloat16)],
        2 * tok_rows * (up_query.size + up_key.size),
        2 * (up_query.size + up_key.size),
        limit=16,
    )(x_index, query_latent, query_first, query_second, up_query, up_key, query_cos, query_sin)

    key_parts = [key_at[:, part * TILE : (part + 1) * TILE] for part in range(2 * len(near))]

    query_at = own_positions.reshape(-1, 1)

    def stage(sources, places, state, last=False):
        return attend(
            queries,
            jnp.concatenate([key_parts[place] for place in places], axis=1),
            query_at,
            sources,
            state,
            up_value if last else None,
        )

    far = [send(part, other_core) for part in near[:3]]
    state = stage(near[:3], [0, 1, 2], ())
    near[3], state = lax.optimization_barrier((near[3], state))
    far.append(send(near[3], other_core))
    state = stage(far[:3], [4, 5, 6], state)
    return stage([near[3], far[3]], [3, 7], state, last=True)


def solution(mesh):
    placed = (
        P("ctx", "head"),
        P("head", None),
        P("head", None),
        P(),
        P(),
        P(None, "head"),
        P(None, "head"),
        P(None, "head"),
        P(),
    )
    return jax.shard_map(
        body, mesh=mesh, in_specs=placed, out_specs=P("ctx", "head"), check_vma=False
    )
```

profile of v0, /device:TPU:1, one launch (start us, length us, event | category | flops | bytes accessed | tf_op | source)
XLA Modules:
  0.0 88.0 jit_solution(17328698014460080225)
XLA Ops:
  0.0 2.6 %shard_map.109 = (f32[144,128]{1,0:T(8,128)}, f32[144,128]{1,0:T(8,128)}, f32[144,128]{1,0:T(8,128)}, f32[144,128]{1,0:T(8,128)}) custom-call(s32[1]{0:T(128)} %bitcast.x_ref, bf16[128,896]{1,0:T(8,128)(2,1)} %hidden, bf16[576,896]{1,0:T(8,128)(2,1)} %bitcast.13), custom_call_target="tpu_custom_call" | custom-call | flops 132120576 | bytes 1032192 | tf_op jit(solution)/shard_map/pallas_call | solution.py:153
  2.6 0.0 copy-start.6
  2.6 2.1 %collective-permute-start = (f32[144,128]{1,0:T(8,128)}, f32[144,128]{1,0:T(8,128)S(1)}, u32[]{:S(2)}, u32[]{:S(2)}) collective-permute-start(f32[144,128]{1,0:T(8,128)} %get-tuple-element.34), channel_id=1, source_target_pairs={{0,1},{8,9},{64,65},{72,73},{128,129},{136,137},{192,193},{200,201... | collective-permute-start | bytes 221192 | tf_op jit(solution)/shard_map/ppermute | solution.py:72
  4.7 2.5 %collective-permute-start.1 = (f32[144,128]{1,0:T(8,128)}, f32[144,128]{1,0:T(8,128)S(1)}, u32[]{:S(2)}, u32[]{:S(2)}) collective-permute-start(f32[144,128]{1,0:T(8,128)} %get-tuple-element.35), channel_id=1, source_target_pairs={{0,2},{8,10},{64,66},{72,74},{128,130},{136,138},{192,194},{200,20... | collective-permute-start | bytes 221192 | tf_op jit(solution)/shard_map/ppermute | solution.py:72
  7.2 1.2 %collective-permute-start.2 = (f32[144,128]{1,0:T(8,128)}, f32[144,128]{1,0:T(8,128)S(1)}, u32[]{:S(2)}, u32[]{:S(2)}) collective-permute-start(f32[144,128]{1,0:T(8,128)} %get-tuple-element.36), channel_id=1, source_target_pairs={{0,3},{8,11},{64,67},{72,75},{128,131},{136,139},{192,195},{200,20... | collective-permute-start | bytes 221192 | tf_op jit(solution)/shard_map/ppermute | solution.py:72
  8.4 0.1 add_multiply_fusion
  8.5 0.8 fusion.16
  9.3 0.1 broadcast_add_fusion.1
  9.4 0.1 add.325
  9.5 0.1 add.335
  9.6 0.1 and_select_fusion.3
  9.6 0.8 select_reduce_fusion
  10.5 0.1 fusion.10
  10.6 0.1 fusion.6
  10.7 0.1 fusion.8.sines
  10.8 0.1 fusion.7
  10.8 0.1 collective-permute-done.2.three
  10.9 0.9 %copy-done.4 = f32[144,128]{1,0:T(8,128)S(1)} copy-done((f32[144,128]{1,0:T(8,128)S(1)}, f32[144,128]{1,0:T(8,128)}, u32[]{:S(2)}) %copy-start.4) | copy-done | bytes 73752
  11.8 7.3 %collective-permute-start.3 = (f32[144,128]{1,0:T(8,128)S(1)}, f32[144,128]{1,0:T(8,128)S(1)}, u32[]{:S(2)}, u32[]{:S(2)}) collective-permute-start(f32[144,128]{1,0:T(8,128)S(1)} %shard_map.110.own), channel_id=1, source_target_pairs={{0,4},{8,12},{64,68},{72,76},{128,132},{136,140},{192,196},{200,20... | collective-permute-start | bytes 221192 | tf_op jit(solution)/shard_map/ppermute | solution.py:72
  19.1 0.1 fusion.9.cosines
  19.2 1.8 %copy-done.1 = bf16[896,1536]{1,0:T(8,128)(2,1)S(1)} copy-done((bf16[896,1536]{1,0:T(8,128)(2,1)S(1)}, bf16[896,1536]{1,0:T(8,128)(2,1)}, u32[]{:S(2)}) %copy-start.1) | copy-done | bytes 2752536
  21.0 0.7 shard_map.112
  21.7 0.0 copy-start.5
  21.7 0.0 collective-permute-done.3.other
  21.7 0.1 shard_map.111.refs_0_
  21.8 0.1 collective-permute-start.4
  21.9 1.5 %collective-permute-start.6 = (f32[384,128]{1,0:T(8,128)S(1)}, f32[384,128]{1,0:T(8,128)S(1)}, u32[]{:S(2)}, u32[]{:S(2)}) collective-permute-start(f32[384,128]{1,0:T(8,128)S(1)} %get-tuple-element.44), channel_id=1, source_target_pairs={{0,1},{8,9},{64,65},{72,73},{128,129},{136,137},{192,193},{200,201... | collective-permute-start | bytes 589832 | tf_op jit(solution)/shard_map/ppermute | solution.py:72
  23.4 1.9 %collective-permute-start.7 = (f32[384,128]{1,0:T(8,128)S(1)}, f32[384,128]{1,0:T(8,128)S(1)}, u32[]{:S(2)}, u32[]{:S(2)}) collective-permute-start(f32[384,128]{1,0:T(8,128)S(1)} %get-tuple-element.45), channel_id=1, source_target_pairs={{0,2},{8,10},{64,66},{72,74},{128,130},{136,138},{192,194},{200,20... | collective-permute-start | bytes 589832 | tf_op jit(solution)/shard_map/ppermute | solution.py:72
  25.3 2.0 %collective-permute-start.8 = (f32[384,128]{1,0:T(8,128)S(1)}, f32[384,128]{1,0:T(8,128)S(1)}, u32[]{:S(2)}, u32[]{:S(2)}) collective-permute-start(f32[384,128]{1,0:T(8,128)S(1)} %get-tuple-element.46), channel_id=1, source_target_pairs={{0,3},{8,11},{64,67},{72,75},{128,131},{136,139},{192,195},{200,20... | collective-permute-start | bytes 589832 | tf_op jit(solution)/shard_map/ppermute | solution.py:72
  27.3 0.0 collective-permute-done.4.refs_1_
  27.3 0.1 collective-permute-start.5
  27.4 0.1 iota_add_fusion
  27.5 0.0 copy-start.2
  27.5 0.1 add.347
  27.6 8.2 %collective-permute-done.5.refs_1_ = bf16[288,128]{1,0:T(8,128)(2,1)S(1)} collective-permute-done((bf16[288,128]{1,0:T(8,128)(2,1)S(1)}, bf16[288,128]{1,0:T(8,128)(2,1)S(1)}, u32[]{:S(2)}, u32[]{:S(2)}) %collective-permute-start.5) | collective-permute-done | bytes 73760 | tf_op jit(solution)/shard_map/ppermute | solution.py:72
  35.8 0.0 collective-permute-done.6.one
  35.8 0.0 collective-permute-done.8.three
  35.9 1.3 %collective-permute-start.11 = (bf16[576,128]{1,0:T(8,128)(2,1)S(1)}, bf16[576,128]{1,0:T(8,128)(2,1)S(1)}, u32[]{:S(2)}, u32[]{:S(2)}) collective-permute-start(bf16[576,128]{1,0:T(8,128)(2,1)S(1)} %shard_map.114.refs_0_), channel_id=1, source_target_pairs={{0,32},{8,140},{64,96},{72,200},{128,160},{136,8},{192,224},{200,7... | collective-permute-start | bytes 442376 | tf_op jit(solution)/shard_map/ppermute | solution.py:72
  37.2 0.0 collective-permute-start.10
  37.2 1.5 %collective-permute-start.9 = (bf16[576,128]{1,0:T(8,128)(2,1)S(1)}, bf16[576,128]{1,0:T(8,128)(2,1)S(1)}, u32[]{:S(2)}, u32[]{:S(2)}) collective-permute-start(bf16[576,128]{1,0:T(8,128)(2,1)S(1)} %shard_map.114.refs_0_), channel_id=1, source_target_pairs={{0,16},{8,72},{64,80},{72,136},{128,144},{136,200},{192,208},{200,... | collective-permute-start | bytes 442376 | tf_op jit(solution)/shard_map/ppermute | solution.py:72
  38.7 2.6 %collective-permute-start.12 = (f32[384,128]{1,0:T(8,128)S(1)}, f32[384,128]{1,0:T(8,128)S(1)}, u32[]{:S(2)}, u32[]{:S(2)}) collective-permute-start(f32[384,128]{1,0:T(8,128)S(1)} %shard_map.115.own), channel_id=1, source_target_pairs={{0,4},{8,12},{64,68},{72,76},{128,132},{136,140},{192,196},{200,20... | collective-permute-start | bytes 589832 | tf_op jit(solution)/shard_map/ppermute | solution.py:72
  41.3 1.4 %collective-permute-done.10.refs_2_ = bf16[576,128]{1,0:T(8,128)(2,1)S(1)} collective-permute-done((bf16[576,128]{1,0:T(8,128)(2,1)S(1)}, bf16[576,128]{1,0:T(8,128)(2,1)S(1)}, u32[]{:S(2)}, u32[]{:S(2)}) %collective-permute-start.10) | collective-permute-done | bytes 147488 | tf_op jit(solution)/shard_map/ppermute | solution.py:72
  42.7 0.0 collective-permute-done.9.refs_1_
  42.8 2.8 %collective-permute-start.17 = (bf16[2304,128]{1,0:T(8,128)(2,1)S(1)}, bf16[2304,128]{1,0:T(8,128)(2,1)S(1)}, u32[]{:S(2)}, u32[]{:S(2)}) collective-permute-start(bf16[2304,128]{1,0:T(8,128)(2,1)S(1)} %shard_map.116.refs_3_), channel_id=1, source_target_pairs={{0,196},{8,56},{64,0},{72,120},{128,64},{136,184},{192,128},{200,2... | collective-permute-start | bytes 1769480 | tf_op jit(solution)/shard_map/ppermute | solution.py:72
  45.6 0.3 fusion.5
  45.9 0.1 copy.16
  46.0 0.1 pad_maximum_fusion.cosines
  46.1 2.9 %collective-permute-done.12.other = f32[384,128]{1,0:T(8,128)S(1)} collective-permute-done((f32[384,128]{1,0:T(8,128)S(1)}, f32[384,128]{1,0:T(8,128)S(1)}, u32[]{:S(2)}, u32[]{:S(2)}) %collective-permute-start.12) | collective-permute-done | bytes 196640 | tf_op jit(solution)/shard_map/ppermute | solution.py:72
  49.0 0.1 shard_map.117.refs_0_.own
  49.2 0.9 %collective-permute-start.13 = (bf16[384,128]{1,0:T(8,128)(2,1)S(1)}, bf16[384,128]{1,0:T(8,128)(2,1)S(1)}, u32[]{:S(2)}, u32[]{:S(2)}) collective-permute-start(bf16[384,128]{1,0:T(8,128)(2,1)S(1)} %shard_map.117.refs_0_.own), channel_id=1, source_target_pairs={{0,1},{8,9},{64,65},{72,73},{128,129},{136,137},{192,193},{200,201... | collective-permute-start | bytes 294920 | tf_op jit(solution)/shard_map/ppermute | solution.py:72
  50.1 0.1 pad_maximum_fusion.1.sines
  50.2 4.6 %collective-permute-start.15 = (bf16[2304,128]{1,0:T(8,128)(2,1)S(1)}, bf16[2304,128]{1,0:T(8,128)(2,1)S(1)}, u32[]{:S(2)}, u32[]{:S(2)}) collective-permute-start(bf16[2304,128]{1,0:T(8,128)(2,1)S(1)} %shard_map.116.refs_3_), channel_id=1, source_target_pairs={{0,132},{8,40},{64,192},{72,104},{128,0},{136,168},{192,68},{200,2... | collective-permute-start | bytes 1769480 | tf_op jit(solution)/shard_map/ppermute | solution.py:72
  54.9 5.7 %collective-permute-start.14 = (bf16[768,128]{1,0:T(8,128)(2,1)S(1)}, bf16[768,128]{1,0:T(8,128)(2,1)S(1)}, u32[]{:S(2)}, u32[]{:S(2)}) collective-permute-start(bf16[768,128]{1,0:T(8,128)(2,1)S(1)} %shard_map.118), channel_id=1, source_target_pairs={{0,3},{8,11},{64,67},{72,75},{128,131},{136,139},{192,195},{200,20... | collective-permute-start | bytes 589832 | tf_op jit(solution)/shard_map/ppermute | solution.py:72
  60.6 1.4 %collective-permute-start.19 = (bf16[2304,128]{1,0:T(8,128)(2,1)S(1)}, bf16[2304,128]{1,0:T(8,128)(2,1)S(1)}, u32[]{:S(2)}, u32[]{:S(2)}) collective-permute-start(bf16[2304,128]{1,0:T(8,128)(2,1)S(1)} %shard_map.116.refs_3_), channel_id=1, source_target_pairs={{0,8},{8,0},{64,72},{72,64},{128,136},{136,128},{192,200},{200,192... | collective-permute-start | bytes 1769480 | tf_op jit(solution)/shard_map/ppermute | solution.py:72
  61.9 1.8 %collective-permute-done.14.second = bf16[768,128]{1,0:T(8,128)(2,1)S(1)} collective-permute-done((bf16[768,128]{1,0:T(8,128)(2,1)S(1)}, bf16[768,128]{1,0:T(8,128)(2,1)S(1)}, u32[]{:S(2)}, u32[]{:S(2)}) %collective-permute-start.14) | collective-permute-done | bytes 196640 | tf_op jit(solution)/shard_map/ppermute | solution.py:72
  63.7 2.3 %copy-done = bf16[1536,1536]{1,0:T(8,128)(2,1)S(1)} copy-done((bf16[1536,1536]{1,0:T(8,128)(2,1)S(1)}, bf16[1536,1536]{1,0:T(8,128)(2,1)}, u32[]{:S(2)}) %copy-start) | copy-done | bytes 4718616
  66.1 2.0 %shard_map.119.refs_0_ = bf16[1024,640]{1,0:T(8,128)(2,1)S(1)} custom-call(s32[1]{0:T(128)} %bitcast.x_ref, bf16[384,128]{1,0:T(8,128)(2,1)S(1)} %shard_map.117.refs_0_.own, bf16[384,128]{1,0:T(8,128)(2,1)S(1)} %collective-permute-done.13.refs_1_.first, bf16[768,128]{1,0:T(8,128)(2,1)S(1)} %collective-permute-done.14.second, bf16[1536,1536]{1,0:T(8,128)(2,1)S(1)} %copy-done, ...), custom_call_target="tpu_custom_call" | custom-call | flops 738197504 | bytes 5767168 | tf_op jit(solution)/shard_map/pallas_call | solution.py:502
  68.1 3.7 %collective-permute-start.21 = (bf16[2304,128]{1,0:T(8,128)(2,1)S(1)}, bf16[2304,128]{1,0:T(8,128)(2,1)S(1)}, u32[]{:S(2)}, u32[]{:S(2)}) collective-permute-start(bf16[2304,128]{1,0:T(8,128)(2,1)S(1)} %collective-permute-done.17.refs_5_), channel_id=1, source_target_pairs={{0,8},{8,0},{64,72},{72,64},{128,136},{136,128},{192,200},{200,192... | collective-permute-start | bytes 1769480 | tf_op jit(solution)/shard_map/ppermute | solution.py:72
  71.8 0.1 collective-permute-start.20
  72.0 4.9 %shard_map.120 = (f32[1024,128]{1,0:T(8,128)S(1)}, f32[1024,128]{1,0:T(8,128)S(1)}, f32[1024,512]{1,0:T(8,128)S(1)}) custom-call(bf16[1024,640]{1,0:T(8,128)(2,1)S(1)} %shard_map.119.refs_0_, s32[1,1536]{1,0:T(1,128)S(1)} %get-tuple-element.66.refs_1_, s32[128,1]{1,0:T(8,128)S(1)} %fusion.1.refs_2_, bf16[2304,128]{1,0:T(8,128)(2,1)S(1)} %shard_map.116.refs_3_, ...), custom_call_target="tpu_custom_call" | custom-call | flops 3623878656 | bytes 3932160 | tf_op jit(solution)/shard_map/pallas_call | solution.py:417
  76.9 0.7 collective-permute-start.18
  77.6 0.0 copy-start.7
  77.6 5.5 %shard_map.121 = (f32[1024,128]{1,0:T(8,128)S(1)}, f32[1024,128]{1,0:T(8,128)S(1)}, f32[1024,512]{1,0:T(8,128)S(1)}) custom-call(bf16[1024,640]{1,0:T(8,128)(2,1)S(1)} %shard_map.119.refs_0_, s32[1,1536]{1,0:T(1,128)S(1)} %get-tuple-element.65.refs_1_, s32[128,1]{1,0:T(8,128)S(1)} %fusion.1.refs_2_, bf16[2304,128]{1,0:T(8,128)(2,1)S(1)} %collective-permute-done.19.refs_3_, ...), custom_call_target="tpu_custom_call" | custom-call | flops 3623878656 | bytes 3932160 | tf_op jit(solution)/shard_map/pallas_call | solution.py:417
  83.1 4.9 %shard_map.122 = bf16[128,1024]{1,0:T(8,128)(2,1)} custom-call(bf16[1024,640]{1,0:T(8,128)(2,1)S(1)} %shard_map.119.refs_0_, s32[1,1024]{1,0:T(1,128)S(1)} %pad_add_fusion.refs_1_, s32[128,1]{1,0:T(8,128)S(1)} %fusion.1.refs_2_, bf16[2304,128]{1,0:T(8,128)(2,1)S(1)} %collective-permute-done.15.refs_3_, ...), custom_call_target="tpu_custom_call" | custom-call | flops 2415919104 | bytes 2621440 | tf_op jit(solution)/shard_map/pallas_call | solution.py:417
  (36 shorter events, 0.3 us)
Async XLA Ops:
  0.0 19.2 %copy-start.3 = (bf16[128,896]{1,0:T(8,128)(2,1)S(1)}, bf16[128,896]{1,0:T(8,128)(2,1)}, u32[]{:S(2)}) copy-start(bf16[128,896]{1,0:T(8,128)(2,1)} %hidden) | copy-start | bytes 688132
  2.6 19.1 %copy-start.6 = (f32[512]{0:T(512)S(1)}, f32[512]{0:T(512)}, u32[]{:S(2)}) copy-start(f32[512]{0:T(512)} %param.15) | copy-start | bytes 6148
  2.6 8.2 %collective-permute-start = (f32[144,128]{1,0:T(8,128)}, f32[144,128]{1,0:T(8,128)S(1)}, u32[]{:S(2)}, u32[]{:S(2)}) collective-permute-start(f32[144,128]{1,0:T(8,128)} %get-tuple-element.34), channel_id=1, source_target_pairs={{0,1},{8,9},{64,65},{72,73},{128,129},{136,137},{192,193},{200,201... | collective-permute-start | bytes 221192 | tf_op jit(solution)/shard_map/ppermute | solution.py:72
  4.7 6.1 %collective-permute-start.1 = (f32[144,128]{1,0:T(8,128)}, f32[144,128]{1,0:T(8,128)S(1)}, u32[]{:S(2)}, u32[]{:S(2)}) collective-permute-start(f32[144,128]{1,0:T(8,128)} %get-tuple-element.35), channel_id=1, source_target_pairs={{0,2},{8,10},{64,66},{72,74},{128,130},{136,138},{192,194},{200,20... | collective-permute-start | bytes 221192 | tf_op jit(solution)/shard_map/ppermute | solution.py:72
  7.2 3.7 %collective-permute-start.2 = (f32[144,128]{1,0:T(8,128)}, f32[144,128]{1,0:T(8,128)S(1)}, u32[]{:S(2)}, u32[]{:S(2)}) collective-permute-start(f32[144,128]{1,0:T(8,128)} %get-tuple-element.36), channel_id=1, source_target_pairs={{0,3},{8,11},{64,67},{72,75},{128,131},{136,139},{192,195},{200,20... | collective-permute-start | bytes 221192 | tf_op jit(solution)/shard_map/ppermute | solution.py:72
  10.9 0.9 %copy-start.4 = (f32[144,128]{1,0:T(8,128)S(1)}, f32[144,128]{1,0:T(8,128)}, u32[]{:S(2)}) copy-start(f32[144,128]{1,0:T(8,128)} %get-tuple-element.33.own) | copy-start | bytes 221188
  11.8 9.9 %collective-permute-start.3 = (f32[144,128]{1,0:T(8,128)S(1)}, f32[144,128]{1,0:T(8,128)S(1)}, u32[]{:S(2)}, u32[]{:S(2)}) collective-permute-start(f32[144,128]{1,0:T(8,128)S(1)} %shard_map.110.own), channel_id=1, source_target_pairs={{0,4},{8,12},{64,68},{72,76},{128,132},{136,140},{192,196},{200,20... | collective-permute-start | bytes 221192 | tf_op jit(solution)/shard_map/ppermute | solution.py:72
  19.2 1.8 %copy-start.1 = (bf16[896,1536]{1,0:T(8,128)(2,1)S(1)}, bf16[896,1536]{1,0:T(8,128)(2,1)}, u32[]{:S(2)}) copy-start(bf16[896,1536]{1,0:T(8,128)(2,1)} %weight.1) | copy-start | bytes 8257540
  21.7 27.4 %copy-start.5 = (f32[1536]{0:T(1024)S(1)}, f32[1536]{0:T(1024)}, u32[]{:S(2)}) copy-start(f32[1536]{0:T(1024)} %param.14) | copy-start | bytes 18436
  21.8 5.4 %collective-permute-start.4 = (bf16[144,128]{1,0:T(8,128)(2,1)S(1)}, bf16[144,128]{1,0:T(8,128)(2,1)S(1)}, u32[]{:S(2)}, u32[]{:S(2)}) collective-permute-start(bf16[144,128]{1,0:T(8,128)(2,1)S(1)} %shard_map.111.refs_0_), channel_id=1, source_target_pairs={{0,1},{8,9},{64,65},{72,73},{128,129},{136,137},{192,193},{200,201... | collective-permute-start | bytes 110600 | tf_op jit(solution)/shard_map/ppermute | solution.py:72
  21.9 13.9 %collective-permute-start.6 = (f32[384,128]{1,0:T(8,128)S(1)}, f32[384,128]{1,0:T(8,128)S(1)}, u32[]{:S(2)}, u32[]{:S(2)}) collective-permute-start(f32[384,128]{1,0:T(8,128)S(1)} %get-tuple-element.44), channel_id=1, source_target_pairs={{0,1},{8,9},{64,65},{72,73},{128,129},{136,137},{192,193},{200,201... | collective-permute-start | bytes 589832 | tf_op jit(solution)/shard_map/ppermute | solution.py:72
  23.4 12.4 %collective-permute-start.7 = (f32[384,128]{1,0:T(8,128)S(1)}, f32[384,128]{1,0:T(8,128)S(1)}, u32[]{:S(2)}, u32[]{:S(2)}) collective-permute-start(f32[384,128]{1,0:T(8,128)S(1)} %get-tuple-element.45), channel_id=1, source_target_pairs={{0,2},{8,10},{64,66},{72,74},{128,130},{136,138},{192,194},{200,20... | collective-permute-start | bytes 589832 | tf_op jit(solution)/shard_map/ppermute | solution.py:72
  25.3 10.6 %collective-permute-start.8 = (f32[384,128]{1,0:T(8,128)S(1)}, f32[384,128]{1,0:T(8,128)S(1)}, u32[]{:S(2)}, u32[]{:S(2)}) collective-permute-start(f32[384,128]{1,0:T(8,128)S(1)} %get-tuple-element.46), channel_id=1, source_target_pairs={{0,3},{8,11},{64,67},{72,75},{128,131},{136,139},{192,195},{200,20... | collective-permute-start | bytes 589832 | tf_op jit(solution)/shard_map/ppermute | solution.py:72
  27.3 8.5 %collective-permute-start.5 = (bf16[288,128]{1,0:T(8,128)(2,1)S(1)}, bf16[288,128]{1,0:T(8,128)(2,1)S(1)}, u32[]{:S(2)}, u32[]{:S(2)}) collective-permute-start(bf16[288,128]{1,0:T(8,128)(2,1)S(1)} %shard_map.113.refs_0_), channel_id=1, source_target_pairs={{0,3},{8,11},{64,67},{72,75},{128,131},{136,139},{192,195},{200,20... | collective-permute-start | bytes 221192 | tf_op jit(solution)/shard_map/ppermute | solution.py:72
  27.5 36.3 %copy-start.2 = (bf16[512,1024]{1,0:T(8,128)(2,1)S(1)}, bf16[512,1024]{1,0:T(8,128)(2,1)}, u32[]{:S(2)}) copy-start(bf16[512,1024]{1,0:T(8,128)(2,1)} %up_key.1) | copy-start | bytes 3145732
  35.9 5.4 %collective-permute-start.11 = (bf16[576,128]{1,0:T(8,128)(2,1)S(1)}, bf16[576,128]{1,0:T(8,128)(2,1)S(1)}, u32[]{:S(2)}, u32[]{:S(2)}) collective-permute-start(bf16[576,128]{1,0:T(8,128)(2,1)S(1)} %shard_map.114.refs_0_), channel_id=1, source_target_pairs={{0,32},{8,140},{64,96},{72,200},{128,160},{136,8},{192,224},{200,7... | collective-permute-start | bytes 442376 | tf_op jit(solution)/shard_map/ppermute | solution.py:72
  37.2 5.5 %collective-permute-start.10 = (bf16[576,128]{1,0:T(8,128)(2,1)S(1)}, bf16[576,128]{1,0:T(8,128)(2,1)S(1)}, u32[]{:S(2)}, u32[]{:S(2)}) collective-permute-start(bf16[576,128]{1,0:T(8,128)(2,1)S(1)} %shard_map.114.refs_0_), channel_id=1, source_target_pairs={{0,48},{8,204},{64,112},{72,8},{128,176},{136,72},{192,240},{200,1... | collective-permute-start | bytes 442376 | tf_op jit(solution)/shard_map/ppermute | solution.py:72
  37.2 5.5 %collective-permute-start.9 = (bf16[576,128]{1,0:T(8,128)(2,1)S(1)}, bf16[576,128]{1,0:T(8,128)(2,1)S(1)}, u32[]{:S(2)}, u32[]{:S(2)}) collective-permute-start(bf16[576,128]{1,0:T(8,128)(2,1)S(1)} %shard_map.114.refs_0_), channel_id=1, source_target_pairs={{0,16},{8,72},{64,80},{72,136},{128,144},{136,200},{192,208},{200,... | collective-permute-start | bytes 442376 | tf_op jit(solution)/shard_map/ppermute | solution.py:72
  38.7 10.3 %collective-permute-start.12 = (f32[384,128]{1,0:T(8,128)S(1)}, f32[384,128]{1,0:T(8,128)S(1)}, u32[]{:S(2)}, u32[]{:S(2)}) collective-permute-start(f32[384,128]{1,0:T(8,128)S(1)} %shard_map.115.own), channel_id=1, source_target_pairs={{0,4},{8,12},{64,68},{72,76},{128,132},{136,140},{192,196},{200,20... | collective-permute-start | bytes 589832 | tf_op jit(solution)/shard_map/ppermute | solution.py:72
  42.8 25.3 %collective-permute-start.17 = (bf16[2304,128]{1,0:T(8,128)(2,1)S(1)}, bf16[2304,128]{1,0:T(8,128)(2,1)S(1)}, u32[]{:S(2)}, u32[]{:S(2)}) collective-permute-start(bf16[2304,128]{1,0:T(8,128)(2,1)S(1)} %shard_map.116.refs_3_), channel_id=1, source_target_pairs={{0,196},{8,56},{64,0},{72,120},{128,64},{136,184},{192,128},{200,2... | collective-permute-start | bytes 1769480 | tf_op jit(solution)/shard_map/ppermute | solution.py:72
  45.6 26.3 %collective-permute-start.16 = (bf16[2304,128]{1,0:T(8,128)(2,1)S(1)}, bf16[2304,128]{1,0:T(8,128)(2,1)S(1)}, u32[]{:S(2)}, u32[]{:S(2)}) collective-permute-start(bf16[2304,128]{1,0:T(8,128)(2,1)S(1)} %shard_map.116.refs_3_), channel_id=1, source_target_pairs={{0,64},{8,24},{64,128},{72,88},{128,192},{136,152},{192,4},{200,21... | collective-permute-start | bytes 1769480 | tf_op jit(solution)/shard_map/ppermute | solution.py:72
  49.2 5.7 %collective-permute-start.13 = (bf16[384,128]{1,0:T(8,128)(2,1)S(1)}, bf16[384,128]{1,0:T(8,128)(2,1)S(1)}, u32[]{:S(2)}, u32[]{:S(2)}) collective-permute-start(bf16[384,128]{1,0:T(8,128)(2,1)S(1)} %shard_map.117.refs_0_.own), channel_id=1, source_target_pairs={{0,1},{8,9},{64,65},{72,73},{128,129},{136,137},{192,193},{200,201... | collective-permute-start | bytes 294920 | tf_op jit(solution)/shard_map/ppermute | solution.py:72
  50.2 26.6 %collective-permute-start.15 = (bf16[2304,128]{1,0:T(8,128)(2,1)S(1)}, bf16[2304,128]{1,0:T(8,128)(2,1)S(1)}, u32[]{:S(2)}, u32[]{:S(2)}) collective-permute-start(bf16[2304,128]{1,0:T(8,128)(2,1)S(1)} %shard_map.116.refs_3_), channel_id=1, source_target_pairs={{0,132},{8,40},{64,192},{72,104},{128,0},{136,168},{192,68},{200,2... | collective-permute-start | bytes 1769480 | tf_op jit(solution)/shard_map/ppermute | solution.py:72
  54.9 8.9 %collective-permute-start.14 = (bf16[768,128]{1,0:T(8,128)(2,1)S(1)}, bf16[768,128]{1,0:T(8,128)(2,1)S(1)}, u32[]{:S(2)}, u32[]{:S(2)}) collective-permute-start(bf16[768,128]{1,0:T(8,128)(2,1)S(1)} %shard_map.118), channel_id=1, source_target_pairs={{0,3},{8,11},{64,67},{72,75},{128,131},{136,139},{192,195},{200,20... | collective-permute-start | bytes 589832 | tf_op jit(solution)/shard_map/ppermute | solution.py:72
  60.6 17.0 %collective-permute-start.19 = (bf16[2304,128]{1,0:T(8,128)(2,1)S(1)}, bf16[2304,128]{1,0:T(8,128)(2,1)S(1)}, u32[]{:S(2)}, u32[]{:S(2)}) collective-permute-start(bf16[2304,128]{1,0:T(8,128)(2,1)S(1)} %shard_map.116.refs_3_), channel_id=1, source_target_pairs={{0,8},{8,0},{64,72},{72,64},{128,136},{136,128},{192,200},{200,192... | collective-permute-start | bytes 1769480 | tf_op jit(solution)/shard_map/ppermute | solution.py:72
  63.7 2.3 %copy-start = (bf16[1536,1536]{1,0:T(8,128)(2,1)S(1)}, bf16[1536,1536]{1,0:T(8,128)(2,1)}, u32[]{:S(2)}) copy-start(bf16[1536,1536]{1,0:T(8,128)(2,1)} %up_query.1) | copy-start | bytes 14155780
  68.1 9.5 %collective-permute-start.21 = (bf16[2304,128]{1,0:T(8,128)(2,1)S(1)}, bf16[2304,128]{1,0:T(8,128)(2,1)S(1)}, u32[]{:S(2)}, u32[]{:S(2)}) collective-permute-start(bf16[2304,128]{1,0:T(8,128)(2,1)S(1)} %collective-permute-done.17.refs_5_), channel_id=1, source_target_pairs={{0,8},{8,0},{64,72},{72,64},{128,136},{136,128},{192,200},{200,192... | collective-permute-start | bytes 1769480 | tf_op jit(solution)/shard_map/ppermute | solution.py:72
  71.8 5.8 %collective-permute-start.20 = (bf16[2304,128]{1,0:T(8,128)(2,1)S(1)}, bf16[2304,128]{1,0:T(8,128)(2,1)S(1)}, u32[]{:S(2)}, u32[]{:S(2)}) collective-permute-start(bf16[2304,128]{1,0:T(8,128)(2,1)S(1)} %collective-permute-done.16.refs_4_), channel_id=1, source_target_pairs={{0,8},{8,0},{64,72},{72,64},{128,136},{136,128},{192,200},{200,192... | collective-permute-start | bytes 1769480 | tf_op jit(solution)/shard_map/ppermute | solution.py:72
  76.9 6.2 %collective-permute-start.18 = (bf16[2304,128]{1,0:T(8,128)(2,1)S(1)}, bf16[2304,128]{1,0:T(8,128)(2,1)S(1)}, u32[]{:S(2)}, u32[]{:S(2)}) collective-permute-start(bf16[2304,128]{1,0:T(8,128)(2,1)S(1)} %collective-permute-done.15.refs_3_), channel_id=1, source_target_pairs={{0,8},{8,0},{64,72},{72,64},{128,136},{136,128},{192,200},{200,192... | collective-permute-start | bytes 1769480 | tf_op jit(solution)/shard_map/ppermute | solution.py:72
  77.6 5.5 %copy-start.7 = (bf16[512,1024]{1,0:T(8,128)(2,1)S(1)}, bf16[512,1024]{1,0:T(8,128)(2,1)}, u32[]{:S(2)}) copy-start(bf16[512,1024]{1,0:T(8,128)(2,1)} %refs_8_.1) | copy-start | bytes 3145732
where the time goes:
time: 88.2 us; the launch traced here: 88 us
  starting transfers between devices  44 us (50%)
  Pallas kernels  20.9 us (24%)
  waiting for transfers between devices  14.4 us (16%)
  local copies, waits for them, and re-layouts  5.43 us (6%)
  other arithmetic  2.98 us (3%)
    ppermute x22, starting transfers between devices, send(): return lax.ppermute(value, AXES, pairs)  44 us
    pallas_call x3, Pallas kernels, attend(): kernel_call(functools.partial(attend_kernel, parts, not state, up_value i...  15.3 us
    ppermute x22, waiting for transfers between devices, send(): return lax.ppermute(value, AXES, pairs)  14.4 us
    unnamed x16, local copies, waits for them, and re-layouts  5.03 us
    pallas_call x1, Pallas kernels, key_down(): kernel_call(key_down_kernel, [jax.ShapeDtypeStruct((PACK, LANES), jnp.flo...  2.6 us
    pallas_call x1, Pallas kernels, body(): kernel_call(query_kernel, jax.ShapeDtypeStruct((local_heads * tok_rows, W...  2.01 us
  transfers between devices with their start and end apart: 22, of which 5 were waited for; matrix products, arithmetic and copies ran while one was open for 4% of the time, Pallas kernels for 15%

commit v1 on v0

--- a/solution.py
+++ b/solution.py
@@ -223,6 +223,33 @@
         size,
         4 * size,
     )(*pieces)
+
+
+def load_kernel(count, *refs):
+    sources, outs, sems = refs[:count], refs[count : 2 * count], refs[2 * count]
+    loads = []
+    for source, out in zip(sources, outs):
+        rows = source.shape[0] // 2
+        for half in range(2):
+            view = pl.ds(half * rows, rows)
+            loads.append(
+                pltpu.make_async_copy(source.at[view], out.at[view], sems.at[len(loads)])
+            )
+    for load in loads:
+        load.start()
+    for load in loads:
+        load.wait()
+
+
+def load_weights(*weights):
+    return kernel_call(
+        functools.partial(load_kernel, len(weights)),
+        [jax.ShapeDtypeStruct(weight.shape, weight.dtype) for weight in weights],
+        [FAR] * len(weights),
+        [pltpu.SemaphoreType.DMA((2 * len(weights),))],
+        0,
+        4 * sum(weight.size for weight in weights),
+    )(*weights)
 
 
 def exchange_halves(values, lanes):
@@ -498,7 +525,11 @@
     key_last, query_latent = lax.optimization_barrier((key_first, query_latent))
     near.append(send(key_last, along_second(-OFFSETS[3])))
     query_first = send(query_latent, pair_x(0))
+    query_first, up_query, up_key = lax.optimization_barrier((query_first, up_query, up_key))
     query_second = send(join([query_latent, query_first], query_rows), pair_x(1))
+    query_second, (up_query, up_key) = lax.optimization_barrier(
+        (query_second, load_weights(up_query, up_key))
+    )
     queries = kernel_call(
         query_kernel,
         jax.ShapeDtypeStruct((local_heads * tok_rows, WIDE), jnp.bfloat16),

time: 88.2 us -> 88.7 us (level)
  starting transfers between devices: 44 us -> 33.4 us
  waiting for transfers between devices: 14.4 us -> 24.3 us
  local copies, waits for them, and re-layouts: 5.43 us -> 6.36 us
    ppermute x22, starting transfers between devices: 44 us -> 33.4 us  [send(): return lax.ppermute(value, AXES, pairs)]
    ppermute x22, waiting for transfers between devices: 14.4 us -> 24.3 us  [send(): return lax.ppermute(value, AXES, pairs)]
    unnamed x16, local copies, waits for them, and re-layouts: 5.03 us -> 5.96 us
  transfers between devices with their start and end apart: 22 -> 22, of which waited for: 5 -> 6; matrix products, arithmetic and copies ran while one was open for 4% -> 4% of each run, Pallas kernels for 15% -> 15%
where the time goes in v1:
time: 88.7 us; the launch traced here: 88.4 us
  starting transfers between devices  33.4 us (38%)
  waiting for transfers between devices  24.3 us (27%)
  Pallas kernels  21 us (24%)
  local copies, waits for them, and re-layouts  6.36 us (7%)
  other arithmetic  2.97 us (3%)
    ppermute x22, starting transfers between devices, send(): return lax.ppermute(value, AXES, pairs)  33.4 us
    ppermute x22, waiting for transfers between devices, send(): return lax.ppermute(value, AXES, pairs)  24.3 us
    pallas_call x3, Pallas kernels, attend(): kernel_call(functools.partial(attend_kernel, parts, not state, up_value i...  15 us
    unnamed x16, local copies, waits for them, and re-layouts  5.96 us
    pallas_call x1, Pallas kernels, key_down(): kernel_call(key_down_kernel, [jax.ShapeDtypeStruct((PACK, LANES), jnp.flo...  2.58 us
    pallas_call x1, Pallas kernels, body(): kernel_call(query_kernel, jax.ShapeDtypeStruct((local_heads * tok_rows, W...  1.97 us
  transfers between devices with their start and end apart: 22, of which 6 were waited for; matrix products, arithmetic and copies ran while one was open for 4% of the time, Pallas kernels for 15%

profile of v1, /device:TPU:1, one launch (start us, length us, event | category | flops | bytes accessed | tf_op | source)
XLA Modules:
  0.0 88.4 jit_solution(9480571825291708055)
XLA Ops:
  0.0 2.6 %shard_map.109 = (f32[144,128]{1,0:T(8,128)}, f32[144,128]{1,0:T(8,128)}, f32[144,128]{1,0:T(8,128)}, f32[144,128]{1,0:T(8,128)}) custom-call(s32[1]{0:T(128)} %bitcast.x_ref, bf16[128,896]{1,0:T(8,128)(2,1)} %hidden, bf16[576,896]{1,0:T(8,128)(2,1)} %bitcast.13), custom_call_target="tpu_custom_call" | custom-call | flops 132120576 | bytes 1032192 | tf_op jit(solution)/shard_map/pallas_call | solution.py:153
  2.6 2.1 %collective-permute-start = (f32[144,128]{1,0:T(8,128)}, f32[144,128]{1,0:T(8,128)S(1)}, u32[]{:S(2)}, u32[]{:S(2)}) collective-permute-start(f32[144,128]{1,0:T(8,128)} %get-tuple-element.42), channel_id=1, source_target_pairs={{0,1},{8,9},{64,65},{72,73},{128,129},{136,137},{192,193},{200,201... | collective-permute-start | bytes 221192 | tf_op jit(solution)/shard_map/ppermute | solution.py:72
  4.7 2.5 %collective-permute-start.1 = (f32[144,128]{1,0:T(8,128)}, f32[144,128]{1,0:T(8,128)S(1)}, u32[]{:S(2)}, u32[]{:S(2)}) collective-permute-start(f32[144,128]{1,0:T(8,128)} %get-tuple-element.43), channel_id=1, source_target_pairs={{0,2},{8,10},{64,66},{72,74},{128,130},{136,138},{192,194},{200,20... | collective-permute-start | bytes 221192 | tf_op jit(solution)/shard_map/ppermute | solution.py:72
  7.2 1.2 %collective-permute-start.2 = (f32[144,128]{1,0:T(8,128)}, f32[144,128]{1,0:T(8,128)S(1)}, u32[]{:S(2)}, u32[]{:S(2)}) collective-permute-start(f32[144,128]{1,0:T(8,128)} %get-tuple-element.44), channel_id=1, source_target_pairs={{0,3},{8,11},{64,67},{72,75},{128,131},{136,139},{192,195},{200,20... | collective-permute-start | bytes 221192 | tf_op jit(solution)/shard_map/ppermute | solution.py:72
  8.3 0.1 add_multiply_fusion
  8.4 0.8 fusion.16
  9.2 0.1 broadcast_add_fusion.1
  9.3 0.1 add.325
  9.4 0.1 add.335
  9.5 0.1 and_select_fusion.3
  9.6 0.7 select_reduce_fusion
  10.4 0.1 fusion.10
  10.6 0.1 fusion.6
  10.6 0.1 fusion.8.sines
  10.7 0.1 fusion.7
  10.8 0.0 collective-permute-done.one
  10.8 0.0 collective-permute-done.1.two
  10.8 0.1 collective-permute-done.2.three
  10.9 0.9 copy-done.4
  11.8 7.3 %collective-permute-start.3 = (f32[144,128]{1,0:T(8,128)S(1)}, f32[144,128]{1,0:T(8,128)S(1)}, u32[]{:S(2)}, u32[]{:S(2)}) collective-permute-start(f32[144,128]{1,0:T(8,128)S(1)} %shard_map.110.own), channel_id=1, source_target_pairs={{0,4},{8,12},{64,68},{72,76},{128,132},{136,140},{192,196},{200,20... | collective-permute-start | bytes 221192 | tf_op jit(solution)/shard_map/ppermute | solution.py:72
  19.1 0.1 fusion.9.cosines
  19.2 1.8 %copy-done.1 = bf16[896,1536]{1,0:T(8,128)(2,1)S(1)} copy-done((bf16[896,1536]{1,0:T(8,128)(2,1)S(1)}, bf16[896,1536]{1,0:T(8,128)(2,1)}, u32[]{:S(2)}) %copy-start.1) | copy-done | bytes 2752536
  21.0 0.9 %copy-done.3 = bf16[128,896]{1,0:T(8,128)(2,1)S(1)} copy-done((bf16[128,896]{1,0:T(8,128)(2,1)S(1)}, bf16[128,896]{1,0:T(8,128)(2,1)}, u32[]{:S(2)}) %copy-start.3) | copy-done | bytes 229400
  21.9 0.6 shard_map.112
  22.6 0.0 copy-start.2
  22.6 0.0 collective-permute-done.3.other
  22.6 0.1 shard_map.111.refs_0_
  22.7 0.1 collective-permute-start.4
  22.8 1.5 %collective-permute-start.6 = (f32[384,128]{1,0:T(8,128)S(1)}, f32[384,128]{1,0:T(8,128)S(1)}, u32[]{:S(2)}, u32[]{:S(2)}) collective-permute-start(f32[384,128]{1,0:T(8,128)S(1)} %get-tuple-element.52), channel_id=1, source_target_pairs={{0,1},{8,9},{64,65},{72,73},{128,129},{136,137},{192,193},{200,201... | collective-permute-start | bytes 589832 | tf_op jit(solution)/shard_map/ppermute | solution.py:72
  24.3 1.9 %collective-permute-start.7 = (f32[384,128]{1,0:T(8,128)S(1)}, f32[384,128]{1,0:T(8,128)S(1)}, u32[]{:S(2)}, u32[]{:S(2)}) collective-permute-start(f32[384,128]{1,0:T(8,128)S(1)} %get-tuple-element.53), channel_id=1, source_target_pairs={{0,2},{8,10},{64,66},{72,74},{128,130},{136,138},{192,194},{200,20... | collective-permute-start | bytes 589832 | tf_op jit(solution)/shard_map/ppermute | solution.py:72
  26.2 2.0 %collective-permute-start.8 = (f32[384,128]{1,0:T(8,128)S(1)}, f32[384,128]{1,0:T(8,128)S(1)}, u32[]{:S(2)}, u32[]{:S(2)}) collective-permute-start(f32[384,128]{1,0:T(8,128)S(1)} %get-tuple-element.54), channel_id=1, source_target_pairs={{0,3},{8,11},{64,67},{72,75},{128,131},{136,139},{192,195},{200,20... | collective-permute-start | bytes 589832 | tf_op jit(solution)/shard_map/ppermute | solution.py:72
  28.2 0.1 collective-permute-start.5
  28.3 0.1 iota_add_fusion
  28.3 0.1 add.347
  28.4 8.2 %collective-permute-done.5.refs_1_ = bf16[288,128]{1,0:T(8,128)(2,1)S(1)} collective-permute-done((bf16[288,128]{1,0:T(8,128)(2,1)S(1)}, bf16[288,128]{1,0:T(8,128)(2,1)S(1)}, u32[]{:S(2)}, u32[]{:S(2)}) %collective-permute-start.5) | collective-permute-done | bytes 73760 | tf_op jit(solution)/shard_map/ppermute | solution.py:72
  36.8 0.1 collective-permute-start.10
  36.9 1.1 %collective-permute-start.11 = (bf16[576,128]{1,0:T(8,128)(2,1)S(1)}, bf16[576,128]{1,0:T(8,128)(2,1)S(1)}, u32[]{:S(2)}, u32[]{:S(2)}) collective-permute-start(bf16[576,128]{1,0:T(8,128)(2,1)S(1)} %shard_map.114.refs_0_), channel_id=1, source_target_pairs={{0,32},{8,140},{64,96},{72,200},{128,160},{136,8},{192,224},{200,7... | collective-permute-start | bytes 442376 | tf_op jit(solution)/shard_map/ppermute | solution.py:72
  38.0 0.3 collective-permute-start.9
  38.3 3.7 %collective-permute-start.12 = (f32[384,128]{1,0:T(8,128)S(1)}, f32[384,128]{1,0:T(8,128)S(1)}, u32[]{:S(2)}, u32[]{:S(2)}) collective-permute-start(f32[384,128]{1,0:T(8,128)S(1)} %shard_map.115.own), channel_id=1, source_target_pairs={{0,4},{8,12},{64,68},{72,76},{128,132},{136,140},{192,196},{200,20... | collective-permute-start | bytes 589832 | tf_op jit(solution)/shard_map/ppermute | solution.py:72
  42.1 0.9 %collective-permute-done.11.refs_3_ = bf16[576,128]{1,0:T(8,128)(2,1)S(1)} collective-permute-done((bf16[576,128]{1,0:T(8,128)(2,1)S(1)}, bf16[576,128]{1,0:T(8,128)(2,1)S(1)}, u32[]{:S(2)}, u32[]{:S(2)}) %collective-permute-start.11) | collective-permute-done | bytes 147488 | tf_op jit(solution)/shard_map/ppermute | solution.py:72
  43.0 9.4 %collective-permute-done.9.refs_1_ = bf16[576,128]{1,0:T(8,128)(2,1)S(1)} collective-permute-done((bf16[576,128]{1,0:T(8,128)(2,1)S(1)}, bf16[576,128]{1,0:T(8,128)(2,1)S(1)}, u32[]{:S(2)}, u32[]{:S(2)}) %collective-permute-start.9) | collective-permute-done | bytes 147488 | tf_op jit(solution)/shard_map/ppermute | solution.py:72
  52.4 0.1 collective-permute-start.16
  52.5 3.6 %collective-permute-start.17 = (bf16[2304,128]{1,0:T(8,128)(2,1)S(1)}, bf16[2304,128]{1,0:T(8,128)(2,1)S(1)}, u32[]{:S(2)}, u32[]{:S(2)}) collective-permute-start(bf16[2304,128]{1,0:T(8,128)(2,1)S(1)} %shard_map.116.refs_3_), channel_id=1, source_target_pairs={{0,196},{8,56},{64,0},{72,120},{128,64},{136,184},{192,128},{200,2... | collective-permute-start | bytes 1769480 | tf_op jit(solution)/shard_map/ppermute | solution.py:72
  56.1 0.3 fusion.5
  56.4 0.1 copy.16
  56.5 0.1 pad_maximum_fusion.cosines
  56.7 0.1 shard_map.117.refs_0_.own
  56.8 0.7 collective-permute-start.13
  57.5 0.1 pad_maximum_fusion.1.sines
  57.6 2.4 %collective-permute-start.15 = (bf16[2304,128]{1,0:T(8,128)(2,1)S(1)}, bf16[2304,128]{1,0:T(8,128)(2,1)S(1)}, u32[]{:S(2)}, u32[]{:S(2)}) collective-permute-start(bf16[2304,128]{1,0:T(8,128)(2,1)S(1)} %shard_map.116.refs_3_), channel_id=1, source_target_pairs={{0,132},{8,40},{64,192},{72,104},{128,0},{136,168},{192,68},{200,2... | collective-permute-start | bytes 1769480 | tf_op jit(solution)/shard_map/ppermute | solution.py:72
  60.0 1.8 %collective-permute-done.13.refs_1_.first = bf16[384,128]{1,0:T(8,128)(2,1)S(1)} collective-permute-done((bf16[384,128]{1,0:T(8,128)(2,1)S(1)}, bf16[384,128]{1,0:T(8,128)(2,1)S(1)}, u32[]{:S(2)}, u32[]{:S(2)}) %collective-permute-start.13) | collective-permute-done | bytes 98336 | tf_op jit(solution)/shard_map/ppermute | solution.py:72
  61.8 0.1 collective-permute-start.14
  62.0 0.6 collective-permute-start.19
  62.5 2.3 %copy-done = bf16[1536,1536]{1,0:T(8,128)(2,1)S(1)} copy-done((bf16[1536,1536]{1,0:T(8,128)(2,1)S(1)}, bf16[1536,1536]{1,0:T(8,128)(2,1)}, u32[]{:S(2)}) %copy-start) | copy-done | bytes 4718616
  64.9 0.4 shard_map.119
  65.3 3.8 %collective-permute-done.14.second = bf16[768,128]{1,0:T(8,128)(2,1)S(1)} collective-permute-done((bf16[768,128]{1,0:T(8,128)(2,1)S(1)}, bf16[768,128]{1,0:T(8,128)(2,1)S(1)}, u32[]{:S(2)}, u32[]{:S(2)}) %collective-permute-start.14) | collective-permute-done | bytes 196640 | tf_op jit(solution)/shard_map/ppermute | solution.py:72
  69.1 2.0 %shard_map.120.refs_0_ = bf16[1024,640]{1,0:T(8,128)(2,1)S(1)} custom-call(s32[1]{0:T(128)} %bitcast.x_ref, bf16[384,128]{1,0:T(8,128)(2,1)S(1)} %shard_map.117.refs_0_.own, bf16[384,128]{1,0:T(8,128)(2,1)S(1)} %collective-permute-done.13.refs_1_.first, bf16[768,128]{1,0:T(8,128)(2,1)S(1)} %collective-permute-done.14.second, ...), custom_call_target="tpu_custom_call" | custom-call | flops 738197504 | bytes 5767168 | tf_op jit(solution)/shard_map/pallas_call | solution.py:533
  71.1 1.4 %collective-permute-start.20 = (bf16[2304,128]{1,0:T(8,128)(2,1)S(1)}, bf16[2304,128]{1,0:T(8,128)(2,1)S(1)}, u32[]{:S(2)}, u32[]{:S(2)}) collective-permute-start(bf16[2304,128]{1,0:T(8,128)(2,1)S(1)} %collective-permute-done.16.refs_4_), channel_id=1, source_target_pairs={{0,8},{8,0},{64,72},{72,64},{128,136},{136,128},{192,200},{200,192... | collective-permute-start | bytes 1769480 | tf_op jit(solution)/shard_map/ppermute | solution.py:72
  72.5 0.1 collective-permute-start.21
  72.6 4.9 %shard_map.121 = (f32[1024,128]{1,0:T(8,128)S(1)}, f32[1024,128]{1,0:T(8,128)S(1)}, f32[1024,512]{1,0:T(8,128)S(1)}) custom-call(bf16[1024,640]{1,0:T(8,128)(2,1)S(1)} %shard_map.120.refs_0_, s32[1,1536]{1,0:T(1,128)S(1)} %get-tuple-element.82.refs_1_, s32[128,1]{1,0:T(8,128)S(1)} %fusion.1.refs_2_, bf16[2304,128]{1,0:T(8,128)(2,1)S(1)} %shard_map.116.refs_3_, ...), custom_call_target="tpu_custom_call" | custom-call | flops 3623878656 | bytes 3932160 | tf_op jit(solution)/shard_map/pallas_call | solution.py:444
  77.5 0.7 collective-permute-start.18
  78.2 0.0 copy-start.7
  78.2 5.3 %shard_map.122 = (f32[1024,128]{1,0:T(8,128)S(1)}, f32[1024,128]{1,0:T(8,128)S(1)}, f32[1024,512]{1,0:T(8,128)S(1)}) custom-call(bf16[1024,640]{1,0:T(8,128)(2,1)S(1)} %shard_map.120.refs_0_, s32[1,1536]{1,0:T(1,128)S(1)} %get-tuple-element.81.refs_1_, s32[128,1]{1,0:T(8,128)S(1)} %fusion.1.refs_2_, bf16[2304,128]{1,0:T(8,128)(2,1)S(1)} %collective-permute-done.19.refs_3_, ...), custom_call_target="tpu_custom_call" | custom-call | flops 3623878656 | bytes 3932160 | tf_op jit(solution)/shard_map/pallas_call | solution.py:444
  83.6 4.8 %shard_map.123 = bf16[128,1024]{1,0:T(8,128)(2,1)} custom-call(bf16[1024,640]{1,0:T(8,128)(2,1)S(1)} %shard_map.120.refs_0_, s32[1,1024]{1,0:T(1,128)S(1)} %pad_add_fusion.refs_1_, s32[128,1]{1,0:T(8,128)S(1)} %fusion.1.refs_2_, bf16[2304,128]{1,0:T(8,128)(2,1)S(1)} %collective-permute-done.15.refs_3_, ...), custom_call_target="tpu_custom_call" | custom-call | flops 2415919104 | bytes 2621440 | tf_op jit(solution)/shard_map/pallas_call | solution.py:444
  (37 shorter events, 0.3 us)
Async XLA Ops:
  0.0 22.6 %copy-start.6 = (f32[512]{0:T(512)S(1)}, f32[512]{0:T(512)}, u32[]{:S(2)}) copy-start(f32[512]{0:T(512)} %param.15) | copy-start | bytes 6148
  2.6 8.2 %collective-permute-start = (f32[144,128]{1,0:T(8,128)}, f32[144,128]{1,0:T(8,128)S(1)}, u32[]{:S(2)}, u32[]{:S(2)}) collective-permute-start(f32[144,128]{1,0:T(8,128)} %get-tuple-element.42), channel_id=1, source_target_pairs={{0,1},{8,9},{64,65},{72,73},{128,129},{136,137},{192,193},{200,201... | collective-permute-start | bytes 221192 | tf_op jit(solution)/shard_map/ppermute | solution.py:72
  4.7 6.1 %collective-permute-start.1 = (f32[144,128]{1,0:T(8,128)}, f32[144,128]{1,0:T(8,128)S(1)}, u32[]{:S(2)}, u32[]{:S(2)}) collective-permute-start(f32[144,128]{1,0:T(8,128)} %get-tuple-element.43), channel_id=1, source_target_pairs={{0,2},{8,10},{64,66},{72,74},{128,130},{136,138},{192,194},{200,20... | collective-permute-start | bytes 221192 | tf_op jit(solution)/shard_map/ppermute | solution.py:72
  7.2 3.7 %collective-permute-start.2 = (f32[144,128]{1,0:T(8,128)}, f32[144,128]{1,0:T(8,128)S(1)}, u32[]{:S(2)}, u32[]{:S(2)}) collective-permute-start(f32[144,128]{1,0:T(8,128)} %get-tuple-element.44), channel_id=1, source_target_pairs={{0,3},{8,11},{64,67},{72,75},{128,131},{136,139},{192,195},{200,20... | collective-permute-start | bytes 221192 | tf_op jit(solution)/shard_map/ppermute | solution.py:72
  10.9 0.9 %copy-start.4 = (f32[144,128]{1,0:T(8,128)S(1)}, f32[144,128]{1,0:T(8,128)}, u32[]{:S(2)}) copy-start(f32[144,128]{1,0:T(8,128)} %get-tuple-element.41.own) | copy-start | bytes 221188
  11.8 10.8 %collective-permute-start.3 = (f32[144,128]{1,0:T(8,128)S(1)}, f32[144,128]{1,0:T(8,128)S(1)}, u32[]{:S(2)}, u32[]{:S(2)}) collective-permute-start(f32[144,128]{1,0:T(8,128)S(1)} %shard_map.110.own), channel_id=1, source_target_pairs={{0,4},{8,12},{64,68},{72,76},{128,132},{136,140},{192,196},{200,20... | collective-permute-start | bytes 221192 | tf_op jit(solution)/shard_map/ppermute | solution.py:72
  19.2 1.8 %copy-start.1 = (bf16[896,1536]{1,0:T(8,128)(2,1)S(1)}, bf16[896,1536]{1,0:T(8,128)(2,1)}, u32[]{:S(2)}) copy-start(bf16[896,1536]{1,0:T(8,128)(2,1)} %weight.1) | copy-start | bytes 8257540
  21.0 0.9 %copy-start.3 = (bf16[128,896]{1,0:T(8,128)(2,1)S(1)}, bf16[128,896]{1,0:T(8,128)(2,1)}, u32[]{:S(2)}) copy-start(bf16[128,896]{1,0:T(8,128)(2,1)} %hidden) | copy-start | bytes 688132
  21.9 34.8 %copy-start.5 = (f32[1536]{0:T(1024)S(1)}, f32[1536]{0:T(1024)}, u32[]{:S(2)}) copy-start(f32[1536]{0:T(1024)} %param.14) | copy-start | bytes 18436
  22.6 40.0 %copy-start.2 = (bf16[512,1024]{1,0:T(8,128)(2,1)S(1)}, bf16[512,1024]{1,0:T(8,128)(2,1)}, u32[]{:S(2)}) copy-start(bf16[512,1024]{1,0:T(8,128)(2,1)} %refs_1_) | copy-start | bytes 3145732
  22.7 5.4 %collective-permute-start.4 = (bf16[144,128]{1,0:T(8,128)(2,1)S(1)}, bf16[144,128]{1,0:T(8,128)(2,1)S(1)}, u32[]{:S(2)}, u32[]{:S(2)}) collective-permute-start(bf16[144,128]{1,0:T(8,128)(2,1)S(1)} %shard_map.111.refs_0_), channel_id=1, source_target_pairs={{0,1},{8,9},{64,65},{72,73},{128,129},{136,137},{192,193},{200,201... | collective-permute-start | bytes 110600 | tf_op jit(solution)/shard_map/ppermute | solution.py:72
  22.8 13.9 %collective-permute-start.6 = (f32[384,128]{1,0:T(8,128)S(1)}, f32[384,128]{1,0:T(8,128)S(1)}, u32[]{:S(2)}, u32[]{:S(2)}) collective-permute-start(f32[384,128]{1,0:T(8,128)S(1)} %get-tuple-element.52), channel_id=1, source_target_pairs={{0,1},{8,9},{64,65},{72,73},{128,129},{136,137},{192,193},{200,201... | collective-permute-start | bytes 589832 | tf_op jit(solution)/shard_map/ppermute | solution.py:72
  24.3 12.5 %collective-permute-start.7 = (f32[384,128]{1,0:T(8,128)S(1)}, f32[384,128]{1,0:T(8,128)S(1)}, u32[]{:S(2)}, u32[]{:S(2)}) collective-permute-start(f32[384,128]{1,0:T(8,128)S(1)} %get-tuple-element.53), channel_id=1, source_target_pairs={{0,2},{8,10},{64,66},{72,74},{128,130},{136,138},{192,194},{200,20... | collective-permute-start | bytes 589832 | tf_op jit(solution)/shard_map/ppermute | solution.py:72
  26.2 10.6 %collective-permute-start.8 = (f32[384,128]{1,0:T(8,128)S(1)}, f32[384,128]{1,0:T(8,128)S(1)}, u32[]{:S(2)}, u32[]{:S(2)}) collective-permute-start(f32[384,128]{1,0:T(8,128)S(1)} %get-tuple-element.54), channel_id=1, source_target_pairs={{0,3},{8,11},{64,67},{72,75},{128,131},{136,139},{192,195},{200,20... | collective-permute-start | bytes 589832 | tf_op jit(solution)/shard_map/ppermute | solution.py:72
  28.2 8.5 %collective-permute-start.5 = (bf16[288,128]{1,0:T(8,128)(2,1)S(1)}, bf16[288,128]{1,0:T(8,128)(2,1)S(1)}, u32[]{:S(2)}, u32[]{:S(2)}) collective-permute-start(bf16[288,128]{1,0:T(8,128)(2,1)S(1)} %shard_map.113.refs_0_), channel_id=1, source_target_pairs={{0,3},{8,11},{64,67},{72,75},{128,131},{136,139},{192,195},{200,20... | collective-permute-start | bytes 221192 | tf_op jit(solution)/shard_map/ppermute | solution.py:72
  36.8 5.3 %collective-permute-start.10 = (bf16[576,128]{1,0:T(8,128)(2,1)S(1)}, bf16[576,128]{1,0:T(8,128)(2,1)S(1)}, u32[]{:S(2)}, u32[]{:S(2)}) collective-permute-start(bf16[576,128]{1,0:T(8,128)(2,1)S(1)} %shard_map.114.refs_0_), channel_id=1, source_target_pairs={{0,48},{8,204},{64,112},{72,8},{128,176},{136,72},{192,240},{200,1... | collective-permute-start | bytes 442376 | tf_op jit(solution)/shard_map/ppermute | solution.py:72
  36.9 6.1 %collective-permute-start.11 = (bf16[576,128]{1,0:T(8,128)(2,1)S(1)}, bf16[576,128]{1,0:T(8,128)(2,1)S(1)}, u32[]{:S(2)}, u32[]{:S(2)}) collective-permute-start(bf16[576,128]{1,0:T(8,128)(2,1)S(1)} %shard_map.114.refs_0_), channel_id=1, source_target_pairs={{0,32},{8,140},{64,96},{72,200},{128,160},{136,8},{192,224},{200,7... | collective-permute-start | bytes 442376 | tf_op jit(solution)/shard_map/ppermute | solution.py:72
  38.0 14.4 %collective-permute-start.9 = (bf16[576,128]{1,0:T(8,128)(2,1)S(1)}, bf16[576,128]{1,0:T(8,128)(2,1)S(1)}, u32[]{:S(2)}, u32[]{:S(2)}) collective-permute-start(bf16[576,128]{1,0:T(8,128)(2,1)S(1)} %shard_map.114.refs_0_), channel_id=1, source_target_pairs={{0,16},{8,72},{64,80},{72,136},{128,144},{136,200},{192,208},{200,... | collective-permute-start | bytes 442376 | tf_op jit(solution)/shard_map/ppermute | solution.py:72
  38.3 18.3 %collective-permute-start.12 = (f32[384,128]{1,0:T(8,128)S(1)}, f32[384,128]{1,0:T(8,128)S(1)}, u32[]{:S(2)}, u32[]{:S(2)}) collective-permute-start(f32[384,128]{1,0:T(8,128)S(1)} %shard_map.115.own), channel_id=1, source_target_pairs={{0,4},{8,12},{64,68},{72,76},{128,132},{136,140},{192,196},{200,20... | collective-permute-start | bytes 589832 | tf_op jit(solution)/shard_map/ppermute | solution.py:72
  52.4 18.6 %collective-permute-start.16 = (bf16[2304,128]{1,0:T(8,128)(2,1)S(1)}, bf16[2304,128]{1,0:T(8,128)(2,1)S(1)}, u32[]{:S(2)}, u32[]{:S(2)}) collective-permute-start(bf16[2304,128]{1,0:T(8,128)(2,1)S(1)} %shard_map.116.refs_3_), channel_id=1, source_target_pairs={{0,64},{8,24},{64,128},{72,88},{128,192},{136,152},{192,4},{200,21... | collective-permute-start | bytes 1769480 | tf_op jit(solution)/shard_map/ppermute | solution.py:72
  52.5 20.0 %collective-permute-start.17 = (bf16[2304,128]{1,0:T(8,128)(2,1)S(1)}, bf16[2304,128]{1,0:T(8,128)(2,1)S(1)}, u32[]{:S(2)}, u32[]{:S(2)}) collective-permute-start(bf16[2304,128]{1,0:T(8,128)(2,1)S(1)} %shard_map.116.refs_3_), channel_id=1, source_target_pairs={{0,196},{8,56},{64,0},{72,120},{128,64},{136,184},{192,128},{200,2... | collective-permute-start | bytes 1769480 | tf_op jit(solution)/shard_map/ppermute | solution.py:72
  56.8 5.0 %collective-permute-start.13 = (bf16[384,128]{1,0:T(8,128)(2,1)S(1)}, bf16[384,128]{1,0:T(8,128)(2,1)S(1)}, u32[]{:S(2)}, u32[]{:S(2)}) collective-permute-start(bf16[384,128]{1,0:T(8,128)(2,1)S(1)} %shard_map.117.refs_0_.own), channel_id=1, source_target_pairs={{0,1},{8,9},{64,65},{72,73},{128,129},{136,137},{192,193},{200,201... | collective-permute-start | bytes 294920 | tf_op jit(solution)/shard_map/ppermute | solution.py:72
  57.6 19.9 %collective-permute-start.15 = (bf16[2304,128]{1,0:T(8,128)(2,1)S(1)}, bf16[2304,128]{1,0:T(8,128)(2,1)S(1)}, u32[]{:S(2)}, u32[]{:S(2)}) collective-permute-start(bf16[2304,128]{1,0:T(8,128)(2,1)S(1)} %shard_map.116.refs_3_), channel_id=1, source_target_pairs={{0,132},{8,40},{64,192},{72,104},{128,0},{136,168},{192,68},{200,2... | collective-permute-start | bytes 1769480 | tf_op jit(solution)/shard_map/ppermute | solution.py:72
  61.8 7.3 %collective-permute-start.14 = (bf16[768,128]{1,0:T(8,128)(2,1)S(1)}, bf16[768,128]{1,0:T(8,128)(2,1)S(1)}, u32[]{:S(2)}, u32[]{:S(2)}) collective-permute-start(bf16[768,128]{1,0:T(8,128)(2,1)S(1)} %shard_map.118), channel_id=1, source_target_pairs={{0,3},{8,11},{64,67},{72,75},{128,131},{136,139},{192,195},{200,20... | collective-permute-start | bytes 589832 | tf_op jit(solution)/shard_map/ppermute | solution.py:72
  62.0 16.3 %collective-permute-start.19 = (bf16[2304,128]{1,0:T(8,128)(2,1)S(1)}, bf16[2304,128]{1,0:T(8,128)(2,1)S(1)}, u32[]{:S(2)}, u32[]{:S(2)}) collective-permute-start(bf16[2304,128]{1,0:T(8,128)(2,1)S(1)} %shard_map.116.refs_3_), channel_id=1, source_target_pairs={{0,8},{8,0},{64,72},{72,64},{128,136},{136,128},{192,200},{200,192... | collective-permute-start | bytes 1769480 | tf_op jit(solution)/shard_map/ppermute | solution.py:72
  62.5 2.3 %copy-start = (bf16[1536,1536]{1,0:T(8,128)(2,1)S(1)}, bf16[1536,1536]{1,0:T(8,128)(2,1)}, u32[]{:S(2)}) copy-start(bf16[1536,1536]{1,0:T(8,128)(2,1)} %refs_0_) | copy-start | bytes 14155780
  71.1 7.1 %collective-permute-start.20 = (bf16[2304,128]{1,0:T(8,128)(2,1)S(1)}, bf16[2304,128]{1,0:T(8,128)(2,1)S(1)}, u32[]{:S(2)}, u32[]{:S(2)}) collective-permute-start(bf16[2304,128]{1,0:T(8,128)(2,1)S(1)} %collective-permute-done.16.refs_4_), channel_id=1, source_target_pairs={{0,8},{8,0},{64,72},{72,64},{128,136},{136,128},{192,200},{200,192... | collective-permute-start | bytes 1769480 | tf_op jit(solution)/shard_map/ppermute | solution.py:72
  72.5 5.7 %collective-permute-start.21 = (bf16[2304,128]{1,0:T(8,128)(2,1)S(1)}, bf16[2304,128]{1,0:T(8,128)(2,1)S(1)}, u32[]{:S(2)}, u32[]{:S(2)}) collective-permute-start(bf16[2304,128]{1,0:T(8,128)(2,1)S(1)} %collective-permute-done.17.refs_5_), channel_id=1, source_target_pairs={{0,8},{8,0},{64,72},{72,64},{128,136},{136,128},{192,200},{200,192... | collective-permute-start | bytes 1769480 | tf_op jit(solution)/shard_map/ppermute | solution.py:72
  77.5 6.1 %collective-permute-start.18 = (bf16[2304,128]{1,0:T(8,128)(2,1)S(1)}, bf16[2304,128]{1,0:T(8,128)(2,1)S(1)}, u32[]{:S(2)}, u32[]{:S(2)}) collective-permute-start(bf16[2304,128]{1,0:T(8,128)(2,1)S(1)} %collective-permute-done.15.refs_3_), channel_id=1, source_target_pairs={{0,8},{8,0},{64,72},{72,64},{128,136},{136,128},{192,200},{200,192... | collective-permute-start | bytes 1769480 | tf_op jit(solution)/shard_map/ppermute | solution.py:72
  78.2 5.3 %copy-start.7 = (bf16[512,1024]{1,0:T(8,128)(2,1)S(1)}, bf16[512,1024]{1,0:T(8,128)(2,1)}, u32[]{:S(2)}) copy-start(bf16[512,1024]{1,0:T(8,128)(2,1)} %refs_8_.1) | copy-start | bytes 3145732

commit v2 on v1

--- a/solution.py
+++ b/solution.py
@@ -522,11 +522,12 @@
         10 * query_half.size,
         10 * query_half.size,
     )(query_half, send(query_half, other_half), query_gain.reshape(-1, LANES))
-    key_last, query_latent = lax.optimization_barrier((key_first, query_latent))
-    near.append(send(key_last, along_second(-OFFSETS[3])))
     query_first = send(query_latent, pair_x(0))
     query_first, up_query, up_key = lax.optimization_barrier((query_first, up_query, up_key))
-    query_second = send(join([query_latent, query_first], query_rows), pair_x(1))
+    query_pair = join([query_latent, query_first], query_rows)
+    key_last, query_pair = lax.optimization_barrier((key_first, query_pair))
+    query_second = send(query_pair, pair_x(1))
+    near.append(send(key_last, along_second(-OFFSETS[3])))
     query_second, (up_query, up_key) = lax.optimization_barrier(
         (query_second, load_weights(up_query, up_key))
     )

time: 88.7 us -> 86.8 us (0.979)
  waiting for transfers between devices: 24.3 us -> 16 us
  starting transfers between devices: 33.4 us -> 39.9 us
    ppermute x22, waiting for transfers between devices: 24.3 us -> 16 us  [send(): return lax.ppermute(value, AXES, pairs)]
    ppermute x22, starting transfers between devices: 33.4 us -> 39.9 us  [send(): return lax.ppermute(value, AXES, pairs)]
  transfers between devices with their start and end apart: 22 -> 22, of which waited for: 6 -> 5; matrix products, arithmetic and copies ran while one was open for 4% -> 4% of each run, Pallas kernels for 15% -> 16%
where the time goes in v2:
time: 86.8 us; the launch traced here: 86.5 us
  starting transfers between devices  39.9 us (46%)
  Pallas kernels  21 us (24%)
  waiting for transfers between devices  16 us (18%)
  local copies, waits for them, and re-layouts  6.36 us (7%)
  other arithmetic  2.97 us (3%)
    ppermute x22, starting transfers between devices, send(): return lax.ppermute(value, AXES, pairs)  39.9 us
    ppermute x22, waiting for transfers between devices, send(): return lax.ppermute(value, AXES, pairs)  16 us
    pallas_call x3, Pallas kernels, attend(): kernel_call(functools.partial(attend_kernel, parts, not state, up_value i...  15 us
    unnamed x16, local copies, waits for them, and re-layouts  5.96 us
    pallas_call x1, Pallas kernels, key_down(): kernel_call(key_down_kernel, [jax.ShapeDtypeStruct((PACK, LANES), jnp.flo...  2.58 us
    pallas_call x1, Pallas kernels, body(): kernel_call(query_kernel, jax.ShapeDtypeStruct((local_heads * tok_rows, W...  1.97 us
  transfers between devices with their start and end apart: 22, of which 5 were waited for; matrix products, arithmetic and copies ran while one was open for 4% of the time, Pallas kernels for 16%

profile of v2, /device:TPU:1, one launch (start us, length us, event | category | flops | bytes accessed | tf_op | source)
XLA Modules:
  0.0 86.5 jit_solution(4113747089086717401)
XLA Ops:
  0.0 2.6 %shard_map.109 = (f32[144,128]{1,0:T(8,128)}, f32[144,128]{1,0:T(8,128)}, f32[144,128]{1,0:T(8,128)}, f32[144,128]{1,0:T(8,128)}) custom-call(s32[1]{0:T(128)} %bitcast.x_ref, bf16[128,896]{1,0:T(8,128)(2,1)} %hidden, bf16[576,896]{1,0:T(8,128)(2,1)} %bitcast.13), custom_call_target="tpu_custom_call" | custom-call | flops 132120576 | bytes 1032192 | tf_op jit(solution)/shard_map/pallas_call | solution.py:153
  2.6 2.1 %collective-permute-start = (f32[144,128]{1,0:T(8,128)}, f32[144,128]{1,0:T(8,128)S(1)}, u32[]{:S(2)}, u32[]{:S(2)}) collective-permute-start(f32[144,128]{1,0:T(8,128)} %get-tuple-element.42), channel_id=1, source_target_pairs={{0,1},{8,9},{64,65},{72,73},{128,129},{136,137},{192,193},{200,201... | collective-permute-start | bytes 221192 | tf_op jit(solution)/shard_map/ppermute | solution.py:72
  4.7 2.5 %collective-permute-start.1 = (f32[144,128]{1,0:T(8,128)}, f32[144,128]{1,0:T(8,128)S(1)}, u32[]{:S(2)}, u32[]{:S(2)}) collective-permute-start(f32[144,128]{1,0:T(8,128)} %get-tuple-element.43), channel_id=1, source_target_pairs={{0,2},{8,10},{64,66},{72,74},{128,130},{136,138},{192,194},{200,20... | collective-permute-start | bytes 221192 | tf_op jit(solution)/shard_map/ppermute | solution.py:72
  7.2 1.2 %collective-permute-start.2 = (f32[144,128]{1,0:T(8,128)}, f32[144,128]{1,0:T(8,128)S(1)}, u32[]{:S(2)}, u32[]{:S(2)}) collective-permute-start(f32[144,128]{1,0:T(8,128)} %get-tuple-element.44), channel_id=1, source_target_pairs={{0,3},{8,11},{64,67},{72,75},{128,131},{136,139},{192,195},{200,20... | collective-permute-start | bytes 221192 | tf_op jit(solution)/shard_map/ppermute | solution.py:72
  8.3 0.1 add_multiply_fusion
  8.4 0.8 fusion.16
  9.2 0.1 broadcast_add_fusion.1
  9.3 0.1 add.325
  9.4 0.1 add.335
  9.5 0.1 and_select_fusion.3
  9.6 0.7 select_reduce_fusion
  10.4 0.1 fusion.10
  10.6 0.1 fusion.6
  10.6 0.1 fusion.8.sines
  10.7 0.1 fusion.7
  10.8 0.0 collective-permute-done.one
  10.8 0.0 collective-permute-done.1.two
  10.8 0.1 collective-permute-done.2.three
  10.9 0.9 %copy-done.4 = f32[144,128]{1,0:T(8,128)S(1)} copy-done((f32[144,128]{1,0:T(8,128)S(1)}, f32[144,128]{1,0:T(8,128)}, u32[]{:S(2)}) %copy-start.4) | copy-done | bytes 73752
  11.8 7.3 %collective-permute-start.3 = (f32[144,128]{1,0:T(8,128)S(1)}, f32[144,128]{1,0:T(8,128)S(1)}, u32[]{:S(2)}, u32[]{:S(2)}) collective-permute-start(f32[144,128]{1,0:T(8,128)S(1)} %shard_map.110.own), channel_id=1, source_target_pairs={{0,4},{8,12},{64,68},{72,76},{128,132},{136,140},{192,196},{200,20... | collective-permute-start | bytes 221192 | tf_op jit(solution)/shard_map/ppermute | solution.py:72
  19.1 0.1 fusion.9.cosines
  19.2 1.8 %copy-done.1 = bf16[896,1536]{1,0:T(8,128)(2,1)S(1)} copy-done((bf16[896,1536]{1,0:T(8,128)(2,1)S(1)}, bf16[896,1536]{1,0:T(8,128)(2,1)}, u32[]{:S(2)}) %copy-start.1) | copy-done | bytes 2752536
  21.0 0.9 %copy-done.3 = bf16[128,896]{1,0:T(8,128)(2,1)S(1)} copy-done((bf16[128,896]{1,0:T(8,128)(2,1)S(1)}, bf16[128,896]{1,0:T(8,128)(2,1)}, u32[]{:S(2)}) %copy-start.3) | copy-done | bytes 229400
  21.9 0.6 shard_map.112
  22.6 0.0 copy-start.2
  22.6 0.1 shard_map.111.refs_0_
  22.7 0.1 collective-permute-start.4
  22.8 1.5 %collective-permute-start.6 = (f32[384,128]{1,0:T(8,128)S(1)}, f32[384,128]{1,0:T(8,128)S(1)}, u32[]{:S(2)}, u32[]{:S(2)}) collective-permute-start(f32[384,128]{1,0:T(8,128)S(1)} %get-tuple-element.52), channel_id=1, source_target_pairs={{0,1},{8,9},{64,65},{72,73},{128,129},{136,137},{192,193},{200,201... | collective-permute-start | bytes 589832 | tf_op jit(solution)/shard_map/ppermute | solution.py:72
  24.3 1.9 %collective-permute-start.7 = (f32[384,128]{1,0:T(8,128)S(1)}, f32[384,128]{1,0:T(8,128)S(1)}, u32[]{:S(2)}, u32[]{:S(2)}) collective-permute-start(f32[384,128]{1,0:T(8,128)S(1)} %get-tuple-element.53), channel_id=1, source_target_pairs={{0,2},{8,10},{64,66},{72,74},{128,130},{136,138},{192,194},{200,20... | collective-permute-start | bytes 589832 | tf_op jit(solution)/shard_map/ppermute | solution.py:72
  26.2 2.0 %collective-permute-start.8 = (f32[384,128]{1,0:T(8,128)S(1)}, f32[384,128]{1,0:T(8,128)S(1)}, u32[]{:S(2)}, u32[]{:S(2)}) collective-permute-start(f32[384,128]{1,0:T(8,128)S(1)} %get-tuple-element.54), channel_id=1, source_target_pairs={{0,3},{8,11},{64,67},{72,75},{128,131},{136,139},{192,195},{200,20... | collective-permute-start | bytes 589832 | tf_op jit(solution)/shard_map/ppermute | solution.py:72
  28.1 0.0 collective-permute-done.4.refs_1_
  28.2 0.1 collective-permute-start.5
  28.3 0.1 iota_add_fusion
  28.3 0.1 add.347
  28.4 8.2 %collective-permute-done.5.refs_1_ = bf16[288,128]{1,0:T(8,128)(2,1)S(1)} collective-permute-done((bf16[288,128]{1,0:T(8,128)(2,1)S(1)}, bf16[288,128]{1,0:T(8,128)(2,1)S(1)}, u32[]{:S(2)}, u32[]{:S(2)}) %collective-permute-start.5) | collective-permute-done | bytes 73760 | tf_op jit(solution)/shard_map/ppermute | solution.py:72
  36.7 0.0 collective-permute-done.7.two
  36.7 0.0 collective-permute-done.8.three
  36.8 0.8 collective-permute-start.11
  37.6 1.9 %collective-permute-start.12 = (bf16[576,128]{1,0:T(8,128)(2,1)S(1)}, bf16[576,128]{1,0:T(8,128)(2,1)S(1)}, u32[]{:S(2)}, u32[]{:S(2)}) collective-permute-start(bf16[576,128]{1,0:T(8,128)(2,1)S(1)} %shard_map.114.refs_0_), channel_id=1, source_target_pairs={{0,48},{8,204},{64,112},{72,8},{128,176},{136,72},{192,240},{200,1... | collective-permute-start | bytes 442376 | tf_op jit(solution)/shard_map/ppermute | solution.py:72
  39.5 2.6 %collective-permute-start.9 = (f32[384,128]{1,0:T(8,128)S(1)}, f32[384,128]{1,0:T(8,128)S(1)}, u32[]{:S(2)}, u32[]{:S(2)}) collective-permute-start(f32[384,128]{1,0:T(8,128)S(1)} %shard_map.115.own), channel_id=1, source_target_pairs={{0,4},{8,12},{64,68},{72,76},{128,132},{136,140},{192,196},{200,20... | collective-permute-start | bytes 589832 | tf_op jit(solution)/shard_map/ppermute | solution.py:72
  42.2 2.3 %collective-permute-done.13.refs_3_ = bf16[576,128]{1,0:T(8,128)(2,1)S(1)} collective-permute-done((bf16[576,128]{1,0:T(8,128)(2,1)S(1)}, bf16[576,128]{1,0:T(8,128)(2,1)S(1)}, u32[]{:S(2)}, u32[]{:S(2)}) %collective-permute-start.13) | collective-permute-done | bytes 147488 | tf_op jit(solution)/shard_map/ppermute | solution.py:72
  44.5 1.4 %collective-permute-start.16 = (bf16[2304,128]{1,0:T(8,128)(2,1)S(1)}, bf16[2304,128]{1,0:T(8,128)(2,1)S(1)}, u32[]{:S(2)}, u32[]{:S(2)}) collective-permute-start(bf16[2304,128]{1,0:T(8,128)(2,1)S(1)} %shard_map.117.refs_3_), channel_id=1, source_target_pairs={{0,64},{8,24},{64,128},{72,88},{128,192},{136,152},{192,4},{200,21... | collective-permute-start | bytes 1769480 | tf_op jit(solution)/shard_map/ppermute | solution.py:72
  45.9 1.5 %collective-permute-start.17 = (bf16[2304,128]{1,0:T(8,128)(2,1)S(1)}, bf16[2304,128]{1,0:T(8,128)(2,1)S(1)}, u32[]{:S(2)}, u32[]{:S(2)}) collective-permute-start(bf16[2304,128]{1,0:T(8,128)(2,1)S(1)} %shard_map.117.refs_3_), channel_id=1, source_target_pairs={{0,196},{8,56},{64,0},{72,120},{128,64},{136,184},{192,128},{200,2... | collective-permute-start | bytes 1769480 | tf_op jit(solution)/shard_map/ppermute | solution.py:72
  47.4 0.3 fusion.5
  47.8 0.1 copy.16
  47.9 0.1 pad_maximum_fusion.cosines
  48.0 2.1 %collective-permute-done.9.other = f32[384,128]{1,0:T(8,128)S(1)} collective-permute-done((f32[384,128]{1,0:T(8,128)S(1)}, f32[384,128]{1,0:T(8,128)S(1)}, u32[]{:S(2)}, u32[]{:S(2)}) %collective-permute-start.9) | collective-permute-done | bytes 196640 | tf_op jit(solution)/shard_map/ppermute | solution.py:72
  50.1 0.1 shard_map.116.refs_0_.own
  50.3 0.8 collective-permute-start.10
  51.0 0.1 pad_maximum_fusion.1.sines
  51.2 3.1 %collective-permute-done.10.refs_1_.first = bf16[384,128]{1,0:T(8,128)(2,1)S(1)} collective-permute-done((bf16[384,128]{1,0:T(8,128)(2,1)S(1)}, bf16[384,128]{1,0:T(8,128)(2,1)S(1)}, u32[]{:S(2)}, u32[]{:S(2)}) %collective-permute-start.10) | collective-permute-done | bytes 98336 | tf_op jit(solution)/shard_map/ppermute | solution.py:72
  54.3 0.7 collective-permute-start.14
  55.0 3.6 %collective-permute-start.15 = (bf16[2304,128]{1,0:T(8,128)(2,1)S(1)}, bf16[2304,128]{1,0:T(8,128)(2,1)S(1)}, u32[]{:S(2)}, u32[]{:S(2)}) collective-permute-start(bf16[2304,128]{1,0:T(8,128)(2,1)S(1)} %shard_map.117.refs_3_), channel_id=1, source_target_pairs={{0,132},{8,40},{64,192},{72,104},{128,0},{136,168},{192,68},{200,2... | collective-permute-start | bytes 1769480 | tf_op jit(solution)/shard_map/ppermute | solution.py:72
  58.7 6.3 %collective-permute-start.19 = (bf16[2304,128]{1,0:T(8,128)(2,1)S(1)}, bf16[2304,128]{1,0:T(8,128)(2,1)S(1)}, u32[]{:S(2)}, u32[]{:S(2)}) collective-permute-start(bf16[2304,128]{1,0:T(8,128)(2,1)S(1)} %shard_map.117.refs_3_), channel_id=1, source_target_pairs={{0,8},{8,0},{64,72},{72,64},{128,136},{136,128},{192,200},{200,192... | collective-permute-start | bytes 1769480 | tf_op jit(solution)/shard_map/ppermute | solution.py:72
  65.0 2.3 %copy-done = bf16[1536,1536]{1,0:T(8,128)(2,1)S(1)} copy-done((bf16[1536,1536]{1,0:T(8,128)(2,1)S(1)}, bf16[1536,1536]{1,0:T(8,128)(2,1)}, u32[]{:S(2)}) %copy-start) | copy-done | bytes 4718616
  67.3 0.4 shard_map.119
  67.8 2.0 %shard_map.120.refs_0_ = bf16[1024,640]{1,0:T(8,128)(2,1)S(1)} custom-call(s32[1]{0:T(128)} %bitcast.x_ref, bf16[384,128]{1,0:T(8,128)(2,1)S(1)} %shard_map.116.refs_0_.own, bf16[384,128]{1,0:T(8,128)(2,1)S(1)} %collective-permute-done.10.refs_1_.first, bf16[768,128]{1,0:T(8,128)(2,1)S(1)} %collective-permute-done.14.second, ...), custom_call_target="tpu_custom_call" | custom-call | flops 738197504 | bytes 5767168 | tf_op jit(solution)/shard_map/pallas_call | solution.py:534
  69.8 0.8 collective-permute-start.20
  70.6 0.1 collective-permute-start.21
  70.7 4.9 %shard_map.121 = (f32[1024,128]{1,0:T(8,128)S(1)}, f32[1024,128]{1,0:T(8,128)S(1)}, f32[1024,512]{1,0:T(8,128)S(1)}) custom-call(bf16[1024,640]{1,0:T(8,128)(2,1)S(1)} %shard_map.120.refs_0_, s32[1,1536]{1,0:T(1,128)S(1)} %get-tuple-element.82.refs_1_, s32[128,1]{1,0:T(8,128)S(1)} %fusion.1.refs_2_, bf16[2304,128]{1,0:T(8,128)(2,1)S(1)} %shard_map.117.refs_3_, ...), custom_call_target="tpu_custom_call" | custom-call | flops 3623878656 | bytes 3932160 | tf_op jit(solution)/shard_map/pallas_call | solution.py:444
  75.6 0.7 collective-permute-start.18
  76.3 0.0 copy-start.7
  76.3 5.3 %shard_map.122 = (f32[1024,128]{1,0:T(8,128)S(1)}, f32[1024,128]{1,0:T(8,128)S(1)}, f32[1024,512]{1,0:T(8,128)S(1)}) custom-call(bf16[1024,640]{1,0:T(8,128)(2,1)S(1)} %shard_map.120.refs_0_, s32[1,1536]{1,0:T(1,128)S(1)} %get-tuple-element.81.refs_1_, s32[128,1]{1,0:T(8,128)S(1)} %fusion.1.refs_2_, bf16[2304,128]{1,0:T(8,128)(2,1)S(1)} %collective-permute-done.19.refs_3_, ...), custom_call_target="tpu_custom_call" | custom-call | flops 3623878656 | bytes 3932160 | tf_op jit(solution)/shard_map/pallas_call | solution.py:444
  81.7 4.8 %shard_map.123 = bf16[128,1024]{1,0:T(8,128)(2,1)} custom-call(bf16[1024,640]{1,0:T(8,128)(2,1)S(1)} %shard_map.120.refs_0_, s32[1,1024]{1,0:T(1,128)S(1)} %pad_add_fusion.refs_1_, s32[128,1]{1,0:T(8,128)S(1)} %fusion.1.refs_2_, bf16[2304,128]{1,0:T(8,128)(2,1)S(1)} %collective-permute-done.15.refs_3_, ...), custom_call_target="tpu_custom_call" | custom-call | flops 2415919104 | bytes 2621440 | tf_op jit(solution)/shard_map/pallas_call | solution.py:444
  (37 shorter events, 0.3 us)
Async XLA Ops:
  0.0 22.6 %copy-start.6 = (f32[512]{0:T(512)S(1)}, f32[512]{0:T(512)}, u32[]{:S(2)}) copy-start(f32[512]{0:T(512)} %param.15) | copy-start | bytes 6148
  2.6 8.2 %collective-permute-start = (f32[144,128]{1,0:T(8,128)}, f32[144,128]{1,0:T(8,128)S(1)}, u32[]{:S(2)}, u32[]{:S(2)}) collective-permute-start(f32[144,128]{1,0:T(8,128)} %get-tuple-element.42), channel_id=1, source_target_pairs={{0,1},{8,9},{64,65},{72,73},{128,129},{136,137},{192,193},{200,201... | collective-permute-start | bytes 221192 | tf_op jit(solution)/shard_map/ppermute | solution.py:72
  4.7 6.1 %collective-permute-start.1 = (f32[144,128]{1,0:T(8,128)}, f32[144,128]{1,0:T(8,128)S(1)}, u32[]{:S(2)}, u32[]{:S(2)}) collective-permute-start(f32[144,128]{1,0:T(8,128)} %get-tuple-element.43), channel_id=1, source_target_pairs={{0,2},{8,10},{64,66},{72,74},{128,130},{136,138},{192,194},{200,20... | collective-permute-start | bytes 221192 | tf_op jit(solution)/shard_map/ppermute | solution.py:72
  7.2 3.7 %collective-permute-start.2 = (f32[144,128]{1,0:T(8,128)}, f32[144,128]{1,0:T(8,128)S(1)}, u32[]{:S(2)}, u32[]{:S(2)}) collective-permute-start(f32[144,128]{1,0:T(8,128)} %get-tuple-element.44), channel_id=1, source_target_pairs={{0,3},{8,11},{64,67},{72,75},{128,131},{136,139},{192,195},{200,20... | collective-permute-start | bytes 221192 | tf_op jit(solution)/shard_map/ppermute | solution.py:72
  10.9 0.9 %copy-start.4 = (f32[144,128]{1,0:T(8,128)S(1)}, f32[144,128]{1,0:T(8,128)}, u32[]{:S(2)}) copy-start(f32[144,128]{1,0:T(8,128)} %get-tuple-element.41.own) | copy-start | bytes 221188
  11.8 10.8 %collective-permute-start.3 = (f32[144,128]{1,0:T(8,128)S(1)}, f32[144,128]{1,0:T(8,128)S(1)}, u32[]{:S(2)}, u32[]{:S(2)}) collective-permute-start(f32[144,128]{1,0:T(8,128)S(1)} %shard_map.110.own), channel_id=1, source_target_pairs={{0,4},{8,12},{64,68},{72,76},{128,132},{136,140},{192,196},{200,20... | collective-permute-start | bytes 221192 | tf_op jit(solution)/shard_map/ppermute | solution.py:72
  19.2 1.8 %copy-start.1 = (bf16[896,1536]{1,0:T(8,128)(2,1)S(1)}, bf16[896,1536]{1,0:T(8,128)(2,1)}, u32[]{:S(2)}) copy-start(bf16[896,1536]{1,0:T(8,128)(2,1)} %weight.1) | copy-start | bytes 8257540
  21.0 0.9 %copy-start.3 = (bf16[128,896]{1,0:T(8,128)(2,1)S(1)}, bf16[128,896]{1,0:T(8,128)(2,1)}, u32[]{:S(2)}) copy-start(bf16[128,896]{1,0:T(8,128)(2,1)} %hidden) | copy-start | bytes 688132
  21.9 28.2 %copy-start.5 = (f32[1536]{0:T(1024)S(1)}, f32[1536]{0:T(1024)}, u32[]{:S(2)}) copy-start(f32[1536]{0:T(1024)} %param.14) | copy-start | bytes 18436
  22.6 42.4 %copy-start.2 = (bf16[512,1024]{1,0:T(8,128)(2,1)S(1)}, bf16[512,1024]{1,0:T(8,128)(2,1)}, u32[]{:S(2)}) copy-start(bf16[512,1024]{1,0:T(8,128)(2,1)} %refs_1_) | copy-start | bytes 3145732
  22.7 5.4 %collective-permute-start.4 = (bf16[144,128]{1,0:T(8,128)(2,1)S(1)}, bf16[144,128]{1,0:T(8,128)(2,1)S(1)}, u32[]{:S(2)}, u32[]{:S(2)}) collective-permute-start(bf16[144,128]{1,0:T(8,128)(2,1)S(1)} %shard_map.111.refs_0_), channel_id=1, source_target_pairs={{0,1},{8,9},{64,65},{72,73},{128,129},{136,137},{192,193},{200,201... | collective-permute-start | bytes 110600 | tf_op jit(solution)/shard_map/ppermute | solution.py:72
  22.8 13.9 %collective-permute-start.6 = (f32[384,128]{1,0:T(8,128)S(1)}, f32[384,128]{1,0:T(8,128)S(1)}, u32[]{:S(2)}, u32[]{:S(2)}) collective-permute-start(f32[384,128]{1,0:T(8,128)S(1)} %get-tuple-element.52), channel_id=1, source_target_pairs={{0,1},{8,9},{64,65},{72,73},{128,129},{136,137},{192,193},{200,201... | collective-permute-start | bytes 589832 | tf_op jit(solution)/shard_map/ppermute | solution.py:72
  24.3 12.5 %collective-permute-start.7 = (f32[384,128]{1,0:T(8,128)S(1)}, f32[384,128]{1,0:T(8,128)S(1)}, u32[]{:S(2)}, u32[]{:S(2)}) collective-permute-start(f32[384,128]{1,0:T(8,128)S(1)} %get-tuple-element.53), channel_id=1, source_target_pairs={{0,2},{8,10},{64,66},{72,74},{128,130},{136,138},{192,194},{200,20... | collective-permute-start | bytes 589832 | tf_op jit(solution)/shard_map/ppermute | solution.py:72
  26.2 10.6 %collective-permute-start.8 = (f32[384,128]{1,0:T(8,128)S(1)}, f32[384,128]{1,0:T(8,128)S(1)}, u32[]{:S(2)}, u32[]{:S(2)}) collective-permute-start(f32[384,128]{1,0:T(8,128)S(1)} %get-tuple-element.54), channel_id=1, source_target_pairs={{0,3},{8,11},{64,67},{72,75},{128,131},{136,139},{192,195},{200,20... | collective-permute-start | bytes 589832 | tf_op jit(solution)/shard_map/ppermute | solution.py:72
  28.2 8.5 %collective-permute-start.5 = (bf16[288,128]{1,0:T(8,128)(2,1)S(1)}, bf16[288,128]{1,0:T(8,128)(2,1)S(1)}, u32[]{:S(2)}, u32[]{:S(2)}) collective-permute-start(bf16[288,128]{1,0:T(8,128)(2,1)S(1)} %shard_map.113.refs_0_), channel_id=1, source_target_pairs={{0,3},{8,11},{64,67},{72,75},{128,131},{136,139},{192,195},{200,20... | collective-permute-start | bytes 221192 | tf_op jit(solution)/shard_map/ppermute | solution.py:72
  36.8 5.4 %collective-permute-start.11 = (bf16[576,128]{1,0:T(8,128)(2,1)S(1)}, bf16[576,128]{1,0:T(8,128)(2,1)S(1)}, u32[]{:S(2)}, u32[]{:S(2)}) collective-permute-start(bf16[576,128]{1,0:T(8,128)(2,1)S(1)} %shard_map.114.refs_0_), channel_id=1, source_target_pairs={{0,16},{8,72},{64,80},{72,136},{128,144},{136,200},{192,208},{200,... | collective-permute-start | bytes 442376 | tf_op jit(solution)/shard_map/ppermute | solution.py:72
  37.6 4.6 %collective-permute-start.12 = (bf16[576,128]{1,0:T(8,128)(2,1)S(1)}, bf16[576,128]{1,0:T(8,128)(2,1)S(1)}, u32[]{:S(2)}, u32[]{:S(2)}) collective-permute-start(bf16[576,128]{1,0:T(8,128)(2,1)S(1)} %shard_map.114.refs_0_), channel_id=1, source_target_pairs={{0,48},{8,204},{64,112},{72,8},{128,176},{136,72},{192,240},{200,1... | collective-permute-start | bytes 442376 | tf_op jit(solution)/shard_map/ppermute | solution.py:72
  39.5 5.0 %collective-permute-start.13 = (bf16[576,128]{1,0:T(8,128)(2,1)S(1)}, bf16[576,128]{1,0:T(8,128)(2,1)S(1)}, u32[]{:S(2)}, u32[]{:S(2)}) collective-permute-start(bf16[576,128]{1,0:T(8,128)(2,1)S(1)} %shard_map.114.refs_0_), channel_id=1, source_target_pairs={{0,32},{8,140},{64,96},{72,200},{128,160},{136,8},{192,224},{200,7... | collective-permute-start | bytes 442376 | tf_op jit(solution)/shard_map/ppermute | solution.py:72
  39.5 10.6 %collective-permute-start.9 = (f32[384,128]{1,0:T(8,128)S(1)}, f32[384,128]{1,0:T(8,128)S(1)}, u32[]{:S(2)}, u32[]{:S(2)}) collective-permute-start(f32[384,128]{1,0:T(8,128)S(1)} %shard_map.115.own), channel_id=1, source_target_pairs={{0,4},{8,12},{64,68},{72,76},{128,132},{136,140},{192,196},{200,20... | collective-permute-start | bytes 589832 | tf_op jit(solution)/shard_map/ppermute | solution.py:72
  44.5 25.2 %collective-permute-start.16 = (bf16[2304,128]{1,0:T(8,128)(2,1)S(1)}, bf16[2304,128]{1,0:T(8,128)(2,1)S(1)}, u32[]{:S(2)}, u32[]{:S(2)}) collective-permute-start(bf16[2304,128]{1,0:T(8,128)(2,1)S(1)} %shard_map.117.refs_3_), channel_id=1, source_target_pairs={{0,64},{8,24},{64,128},{72,88},{128,192},{136,152},{192,4},{200,21... | collective-permute-start | bytes 1769480 | tf_op jit(solution)/shard_map/ppermute | solution.py:72
  45.9 24.7 %collective-permute-start.17 = (bf16[2304,128]{1,0:T(8,128)(2,1)S(1)}, bf16[2304,128]{1,0:T(8,128)(2,1)S(1)}, u32[]{:S(2)}, u32[]{:S(2)}) collective-permute-start(bf16[2304,128]{1,0:T(8,128)(2,1)S(1)} %shard_map.117.refs_3_), channel_id=1, source_target_pairs={{0,196},{8,56},{64,0},{72,120},{128,64},{136,184},{192,128},{200,2... | collective-permute-start | bytes 1769480 | tf_op jit(solution)/shard_map/ppermute | solution.py:72
  50.3 4.0 %collective-permute-start.10 = (bf16[384,128]{1,0:T(8,128)(2,1)S(1)}, bf16[384,128]{1,0:T(8,128)(2,1)S(1)}, u32[]{:S(2)}, u32[]{:S(2)}) collective-permute-start(bf16[384,128]{1,0:T(8,128)(2,1)S(1)} %shard_map.116.refs_0_.own), channel_id=1, source_target_pairs={{0,1},{8,9},{64,65},{72,73},{128,129},{136,137},{192,193},{200,201... | collective-permute-start | bytes 294920 | tf_op jit(solution)/shard_map/ppermute | solution.py:72
  54.3 13.5 %collective-permute-start.14 = (bf16[768,128]{1,0:T(8,128)(2,1)S(1)}, bf16[768,128]{1,0:T(8,128)(2,1)S(1)}, u32[]{:S(2)}, u32[]{:S(2)}) collective-permute-start(bf16[768,128]{1,0:T(8,128)(2,1)S(1)} %shard_map.118), channel_id=1, source_target_pairs={{0,3},{8,11},{64,67},{72,75},{128,131},{136,139},{192,195},{200,20... | collective-permute-start | bytes 589832 | tf_op jit(solution)/shard_map/ppermute | solution.py:72
  55.0 20.6 %collective-permute-start.15 = (bf16[2304,128]{1,0:T(8,128)(2,1)S(1)}, bf16[2304,128]{1,0:T(8,128)(2,1)S(1)}, u32[]{:S(2)}, u32[]{:S(2)}) collective-permute-start(bf16[2304,128]{1,0:T(8,128)(2,1)S(1)} %shard_map.117.refs_3_), channel_id=1, source_target_pairs={{0,132},{8,40},{64,192},{72,104},{128,0},{136,168},{192,68},{200,2... | collective-permute-start | bytes 1769480 | tf_op jit(solution)/shard_map/ppermute | solution.py:72
  58.7 17.6 %collective-permute-start.19 = (bf16[2304,128]{1,0:T(8,128)(2,1)S(1)}, bf16[2304,128]{1,0:T(8,128)(2,1)S(1)}, u32[]{:S(2)}, u32[]{:S(2)}) collective-permute-start(bf16[2304,128]{1,0:T(8,128)(2,1)S(1)} %shard_map.117.refs_3_), channel_id=1, source_target_pairs={{0,8},{8,0},{64,72},{72,64},{128,136},{136,128},{192,200},{200,192... | collective-permute-start | bytes 1769480 | tf_op jit(solution)/shard_map/ppermute | solution.py:72
  65.0 2.3 %copy-start = (bf16[1536,1536]{1,0:T(8,128)(2,1)S(1)}, bf16[1536,1536]{1,0:T(8,128)(2,1)}, u32[]{:S(2)}) copy-start(bf16[1536,1536]{1,0:T(8,128)(2,1)} %refs_0_) | copy-start | bytes 14155780
  69.8 6.5 %collective-permute-start.20 = (bf16[2304,128]{1,0:T(8,128)(2,1)S(1)}, bf16[2304,128]{1,0:T(8,128)(2,1)S(1)}, u32[]{:S(2)}, u32[]{:S(2)}) collective-permute-start(bf16[2304,128]{1,0:T(8,128)(2,1)S(1)} %collective-permute-done.16.refs_4_), channel_id=1, source_target_pairs={{0,8},{8,0},{64,72},{72,64},{128,136},{136,128},{192,200},{200,192... | collective-permute-start | bytes 1769480 | tf_op jit(solution)/shard_map/ppermute | solution.py:72
  70.6 5.7 %collective-permute-start.21 = (bf16[2304,128]{1,0:T(8,128)(2,1)S(1)}, bf16[2304,128]{1,0:T(8,128)(2,1)S(1)}, u32[]{:S(2)}, u32[]{:S(2)}) collective-permute-start(bf16[2304,128]{1,0:T(8,128)(2,1)S(1)} %collective-permute-done.17.refs_5_), channel_id=1, source_target_pairs={{0,8},{8,0},{64,72},{72,64},{128,136},{136,128},{192,200},{200,192... | collective-permute-start | bytes 1769480 | tf_op jit(solution)/shard_map/ppermute | solution.py:72
  75.6 6.1 %collective-permute-start.18 = (bf16[2304,128]{1,0:T(8,128)(2,1)S(1)}, bf16[2304,128]{1,0:T(8,128)(2,1)S(1)}, u32[]{:S(2)}, u32[]{:S(2)}) collective-permute-start(bf16[2304,128]{1,0:T(8,128)(2,1)S(1)} %collective-permute-done.15.refs_3_), channel_id=1, source_target_pairs={{0,8},{8,0},{64,72},{72,64},{128,136},{136,128},{192,200},{200,192... | collective-permute-start | bytes 1769480 | tf_op jit(solution)/shard_map/ppermute | solution.py:72
  76.3 5.3 %copy-start.7 = (bf16[512,1024]{1,0:T(8,128)(2,1)S(1)}, bf16[512,1024]{1,0:T(8,128)(2,1)}, u32[]{:S(2)}) copy-start(bf16[512,1024]{1,0:T(8,128)(2,1)} %refs_8_.1) | copy-start | bytes 3145732
